TPU v7x, 768 devices: a whole 4x8x12 slice. The times are simulated.
768 devices in a mesh: lon: 192 (over y_hi, x, z, core), lat: 4 (over y_lo).
Axes of the slice: x: 4, y: 8 (y_hi: 2, y_lo: 4; y = y_hi * 4 + y_lo), z: 12, core: 2. Of those that a mesh axis runs over, the one named last changes fastest.
Arguments:
- gen_prev: float32 [3, 384, 64, 64], P(None, 'lon', 'lat'), may hold values from -3 to 3
- gen_cur: float32 [3, 384, 64, 64], P(None, 'lon', 'lat'), may hold values from -3 to 3
- corr_prev: float32 [3, 384, 64, 64], P(None, 'lon', 'lat'), may hold values from -3 to 3
- corr_cur: float32 [3, 384, 64, 64], P(None, 'lon', 'lat'), may hold values from -3 to 3
- adj_prev: float32 [6, 384, 64, 64], P(None, 'lon', 'lat'), may hold values from -3 to 3
- adj_cur: float32 [6, 384, 64, 64], P(None, 'lon', 'lat'), may hold values from -3 to 3
- courant: float32 [384, 64, 64], P('lon', 'lat'), may hold values from 0.05 to 0.3
- noise: float32 [384, 64, 64], P('lon', 'lat'), may hold values from 0.2 to 2
- station_owner: int32 [256], replicated, may hold values from 0 to 191
- station_cell: int32 [256], replicated, may hold values from 0 to 8191
- pairs: int32 [2, 1024], replicated, may hold values from 0 to 255
- observed: float32 [4, 3, 1024], replicated, may hold values from -3 to 3
- checkpoint: int32 [1], replicated, may hold values from 0 to 255
Outputs:
- corr_last: float32 [3, 384, 64, 64], P(None, 'lon', 'lat')
- adjoint: float32 [6, 384, 64, 64], P(None, 'lon', 'lat')
- kernel: float32 [384, 64, 64], P('lon', 'lat')
All inputs are finite; a program needn't handle non-finite values.
Results may differ from a plain program's by a relative error of at most 0.0001.
Values sent between devices are 32-bit elements; how exact they have to be, the bound alone decides.
A program may use at most 32 MiB of HBM per device.

v0:
```python
import jax
import jax.numpy as jnp
from jax import lax
from jax.experimental import pallas as pl
from jax.experimental.pallas import tpu as pltpu
from jax.sharding import PartitionSpec as P

OMEGA = 0.7
MESH = pl.DeviceIdType.MESH
F32 = jnp.float32
BF16 = jnp.bfloat16
LONS = 192
LATS = 4
RING_Z = 12
LONG = 2
ROWS = 16
DEEP = 64
TOTAL_LON = LONS * LONG
ROUND = 24
STEPS = 4
STATIONS = 256
PAIRS = 1024
STRIPS = (-1, 0, 1)
OFFSETS = (-2, -1, 0, 1, 2)
GROUPS = ("xc", "y", "z")
PEERS = {"xc": 7, "y": 7, "z": 11}


def place():
    lon = lax.axis_index("lon")
    lat = lax.axis_index("lat")
    return lon, lat, lon // 24, lon % 24


def peer(group, r):
    lon, lat, block, inner = place()
    if group == "xc":
        t = (block % 4 * 2 + inner % 2 + r) % 8
        return ((block // 4 * 4 + t // 2) * 24 + inner // 2 * 2 + t % 2, lat)
    if group == "y":
        t = (block // 4 * 4 + lat + r) % 8
        return ((t // 4 * 4 + block % 4) * 24 + inner, t % 4)
    return (block * 24 + (inner + 2 * r) % 24, lat)


def split2(v):
    high = v.astype(BF16)
    return high, (v - high.astype(F32)).astype(BF16)


def split3(v):
    high = v.astype(BF16)
    rest = v - high.astype(F32)
    mid = rest.astype(BF16)
    return high, mid, (rest - mid.astype(F32)).astype(BF16)


def dot(a, b):
    return lax.dot_general(a, b, (((1,), (0,)), ((), ())), preferred_element_type=F32)


def dot_t(a, b):
    return lax.dot_general(a, b, (((1,), (1,)), ((), ())), preferred_element_type=F32)


def laplace(cur, p, lane):
    x = cur.get(p)
    low = cur.get(p - 1)
    high = cur.get(p + 1)
    zero = jnp.zeros((ROUND, 128), F32)
    sides = jnp.where(
        lane >= DEEP, zero if low is None else low, zero if high is None else high
    )
    if x is None:
        return pltpu.roll(sides, DEEP, 1)
    along_lon = pltpu.roll(x + sides, DEEP, 1)
    deeper = jnp.where(lane % DEEP == 0, 0.0, pltpu.roll(x, 1, 1))
    higher = jnp.where(lane % DEEP == DEEP - 1, 0.0, pltpu.roll(x, 127, 1))
    north = pltpu.roll(x, 1, 0)
    south = pltpu.roll(x, ROUND - 1, 0)
    return along_lon + (north + south + deeper + higher) - 6.0 * x


def advance(cur, old, speed, pairs, lane):
    new = {}
    for p in pairs:
        v = speed[p] * laplace(cur, p, lane)
        if p in cur:
            v = v + 2.0 * cur[p]
        if p in old:
            v = v - old[p]
        new[p] = v
    return new


def body(
    gen_prev,
    gen_cur,
    corr_prev,
    corr_cur,
    adj_prev,
    adj_cur,
    courant,
    noise,
    owner,
    cell,
    pairs,
    observed,
    checkpoint,
    out_corr,
    out_adj,
    out_kernel,
    st_fields,
    st_cn,
    v_owner,
    v_cell,
    v_pairs,
    v_obs,
    e0,
    e1,
    e2,
    e3,
    e4,
    c0,
    c1,
    c2,
    c3,
    c4,
    cn_strip,
    strip_out,
    strip_in,
    row_out,
    row_in,
    snap,
    adj_one,
    depth_hot,
    first_hot,
    second_hot,
    obs,
    chunks,
    total,
    slots,
    gathered,
    rec,
    load_sem,
    cn_sem,
    bulk_sem,
    group_sem,
):
    lon, lat, block, inner = place()
    ext = {-2: e0, -1: e1, 0: e2, 1: e3, 2: e4}
    cn = {-2: c0, -1: c1, 0: c2, 1: c3, 2: c4}
    loads = []
    sources = [
        (courant, st_cn.at[0]),
        (noise, st_cn.at[1]),
        (gen_cur, st_fields.at[0, pl.ds(0, 3)]),
        (corr_cur, st_fields.at[0, pl.ds(3, 3)]),
        (gen_prev, st_fields.at[1, pl.ds(0, 3)]),
        (corr_prev, st_fields.at[1, pl.ds(3, 3)]),
        (adj_cur, st_fields.at[0, pl.ds(6, 6)]),
        (adj_prev, st_fields.at[1, pl.ds(6, 6)]),
        (owner, v_owner),
        (cell, v_cell),
        (pairs, v_pairs),
        (observed, v_obs),
    ]
    for i, (src, dst) in enumerate(sources):
        copy = pltpu.make_async_copy(src, dst, load_sem.at[i])
        copy.start()
        loads.append(copy)
    barrier = pltpu.get_barrier_semaphore()
    greeted = 0
    for dl in OFFSETS:
        for da in STRIPS:
            if dl or da:
                pl.semaphore_signal(
                    barrier,
                    inc=1,
                    device_id=((lon + dl + LONS) % LONS, (lat + da + LATS) % LATS),
                    device_id_type=MESH,
                )
                greeted += 1
    for group in GROUPS:

        def greet(r, carry, group=group):
            pl.semaphore_signal(barrier, inc=1, device_id=peer(group, r), device_id_type=MESH)
            return carry

        lax.fori_loop(1, PEERS[group] + 1, greet, 0)
        greeted += PEERS[group]

    lane = lax.broadcasted_iota(jnp.int32, (ROUND, 128), 1)
    sub8 = lax.broadcasted_iota(jnp.int32, (8, 128), 0)
    zeros8 = jnp.zeros((8, 128), F32)

    loads[0].wait()
    loads[1].wait()
    for ch in range(2):
        c2[ch, 0:ROWS] = jnp.concatenate([st_cn[ch, 0], st_cn[ch, 1]], axis=1)
    for k in range(2, 8):
        loads[k].wait()

    def pack(ch, carry):
        for t in range(2):
            wide = jnp.concatenate([st_fields[t, ch, 0], st_fields[t, ch, 1]], axis=1)
            e2[t, ch, 0:ROWS] = wide
        now = e2[0, ch, 0:ROWS]
        old = e2[1, ch, 0:ROWS]
        strip_out[0, ch] = jnp.where(sub8 < 4, now[0:8], pltpu.roll(old[0:8], 4, 0))
        strip_out[1, ch] = jnp.where(sub8 < 4, pltpu.roll(now[8:16], 4, 0), old[8:16])
        row_out[0, pl.ds(ch, 1)] = now[0:1]
        row_out[1, pl.ds(ch, 1)] = now[ROWS - 1 : ROWS]
        return carry

    lax.fori_loop(0, 12, pack, 0)
    for k in range(8, 12):
        loads[k].wait()

    pl.semaphore_wait(barrier, greeted)

    has_low = lat > 0
    has_high = lat < LATS - 1

    def target(dl, da):
        return ((lon + dl + LONS) % LONS, (lat + da + LATS) % LATS)

    def remote(src, dst, sems, k, dl, da):
        return pltpu.make_async_remote_copy(
            src, dst, sems.at[0, k], sems.at[1, k], device_id=target(dl, da), device_id_type=MESH
        )

    cn_copies = []
    for dl in (-1, 1, -2, 2):
        cn_copies.append(
            (
                remote(
                    c2.at[:, pl.ds(0, ROWS)],
                    cn[-dl].at[:, pl.ds(0, ROWS)],
                    cn_sem,
                    len(cn_copies),
                    dl,
                    0,
                ),
                0,
            )
        )
    for dl in (0, -1, 1, -2, 2):
        for da in (-1, 1):
            cn_copies.append(
                (
                    remote(
                        c2.at[:, pl.ds(0 if da < 0 else 8, 8)],
                        cn_strip.at[0 if da < 0 else 1, 2 - dl],
                        cn_sem,
                        len(cn_copies),
                        dl,
                        da,
                    ),
                    da,
                )
            )
    bulk = []
    for dl in (-1, 1, -2, 2):
        bulk.append(
            (
                remote(
                    e2.at[:, :, pl.ds(0, ROWS)],
                    ext[-dl].at[:, :, pl.ds(0, ROWS)],
                    bulk_sem,
                    len(bulk),
                    dl,
                    0,
                ),
                0,
            )
        )
    for dl in (0, -1, 1):
        for da in (-1, 1):
            d = 0 if da < 0 else 1
            bulk.append(
                (
                    remote(strip_out.at[d], strip_in.at[d, 1 - dl], bulk_sem, len(bulk), dl, da),
                    da,
                )
            )
    for dl in (-2, 2):
        for da in (-1, 1):
            d = 0 if da < 0 else 1
            bulk.append(
                (
                    remote(
                        row_out.at[d],
                        row_in.at[d, 0 if dl > 0 else 1],
                        bulk_sem,
                        len(bulk),
                        dl,
                        da,
                    ),
                    da,
                )
            )

    def sends(da):
        return has_low if da < 0 else has_high

    def receives(da):
        return has_high if da < 0 else has_low

    for copies in (cn_copies, bulk):
        for copy, da in copies:
            if da:
                pl.when(sends(da))(copy.start)
            else:
                copy.start()

    def take(copies):
        for copy, da in copies:
            if da:
                pl.when(receives(da))(copy.wait_recv)
            else:
                copy.wait_recv()

    own = v_owner[...]
    where_in = v_cell[...]
    slon = own * LONG + where_in // (LATS * ROWS * DEEP)
    slat = where_in // DEEP % (LATS * ROWS)
    slane = where_in // (LATS * ROWS * DEEP) * DEEP + where_in % DEEP
    rel_lon = (slon - lon * LONG + 4 + TOTAL_LON) % TOTAL_LON
    rel_lat = slat - lat * ROWS
    near = (rel_lon < 10) & (rel_lat >= -4) & (rel_lat < ROWS + 4)
    row24 = jnp.where(rel_lat < 0, rel_lat + ROUND, rel_lat)
    spot = jnp.where(near, rel_lon // 2 * ROUND + row24, -1)
    spot = jnp.broadcast_to(spot, (ROUND, STATIONS))
    row_id = lax.broadcasted_iota(jnp.int32, (ROUND, STATIONS), 0)
    lanes = lax.broadcasted_iota(jnp.int32, (128, STATIONS), 0)
    hot = jnp.where(lanes == slane, 1.0, 0.0).astype(BF16)
    depth_hot[0:128] = hot
    depth_hot[128:256] = hot

    phase = checkpoint[0].astype(F32)
    weights = [jnp.cos(jnp.full((ROUND, 128), OMEGA * (phase + n), F32)) for n in range(STEPS)]

    take(cn_copies)
    for p in OFFSETS:
        for ch in range(2):
            above = jnp.where(has_high, cn_strip[0, p + 2, ch], zeros8)
            below = jnp.where(has_low, cn_strip[1, p + 2, ch], zeros8)
            cn[p][ch, ROWS:ROUND] = jnp.where(sub8 < 4, above, below)
    reach = ((-1, 0, 1), (-1, 0, 1), OFFSETS, OFFSETS)

    def responses(i, carry):
        pad = jnp.zeros((8, 128), F32)

        def own_cells(t, ch):
            return jnp.concatenate([e2[t, ch, 0:ROWS], pad], axis=0)

        speed = {p: cn[p][0] for p in OFFSETS}
        gen = {0: own_cells(0, i)}
        gen_old = {0: own_cells(1, i)}
        corr = {0: own_cells(0, 3 + i)}
        corr_old = {0: own_cells(1, 3 + i)}
        for n in range(STEPS):
            gen_new = advance(gen, gen_old, speed, reach[n], lane)
            corr_new = advance(corr, corr_old, speed, reach[n], lane)
            for p in reach[n]:
                if p in gen:
                    corr_new[p] = corr_new[p] + (cn[p][1] * weights[n]) * gen[p]
            gen_old, gen = gen, gen_new
            corr_old, corr = corr, corr_new
            tiles = [field[p] for field in (gen, corr) for p in reach[n]]
            stack = jnp.concatenate(tiles, axis=0)
            picked = dot(jnp.concatenate(split2(stack), axis=1), depth_hot[...])
            for f in range(2):
                summed = jnp.zeros((ROUND, STATIONS), F32)
                for k, p in enumerate(reach[n]):
                    at = (f * len(reach[n]) + k) * ROUND
                    summed = summed + jnp.where(
                        spot == row_id + (p + 2) * ROUND, picked[at : at + ROUND], 0.0
                    )
                line = jnp.sum(summed, axis=0, keepdims=True)
                chunks[2 * n + f, pl.ds(i, 1)] = line[:, 0:128]
                chunks[2 * n + f, pl.ds(3 + i, 1)] = line[:, 128:256]
        return carry

    for j in range(8):
        chunks[j, 6:8] = jnp.zeros((2, 128), F32)
    lax.fori_loop(0, 3, responses, 0)

    me_xc = block % 4 * 2 + inner % 2

    def post(k, group, src_of, dst_of):
        def one(r, carry):
            pltpu.make_async_remote_copy(
                src_of(r),
                dst_of(r),
                group_sem.at[0, k],
                group_sem.at[1, k],
                device_id=peer(group, r),
                device_id_type=MESH,
            ).start()
            return carry

        lax.fori_loop(1, PEERS[group] + 1, one, 0)

    def drain(k, group, side):
        ref = slots.at[k % 3, pl.ds(0, PEERS[group])]
        pltpu.make_async_copy(ref, ref, group_sem.at[side, k]).wait()

    post(0, "xc", lambda r: chunks.at[(me_xc + r) % 8], lambda r: slots.at[0, r - 1])

    take(bulk)

    def assemble(ch, carry):
        for p in STRIPS:
            above = jnp.where(has_high, strip_in[0, p + 1, ch], zeros8)
            below = jnp.where(has_low, strip_in[1, p + 1, ch], zeros8)
            ext[p][0, ch, ROWS:ROUND] = jnp.where(sub8 < 4, above, pltpu.roll(below, 4, 0))
            ext[p][1, ch, ROWS:ROUND] = jnp.where(sub8 < 4, pltpu.roll(above, 4, 0), below)
        for k, p in enumerate((-2, 2)):
            above = jnp.where(has_high, row_in[0, k, pl.ds(ch, 1)], 0.0)
            below = jnp.where(has_low, row_in[1, k, pl.ds(ch, 1)], 0.0)
            ext[p][0, ch, ROWS:ROUND] = jnp.where(
                sub8 == 0, above, jnp.where(sub8 == 7, below, 0.0)
            )
            ext[p][1, ch, ROWS:ROUND] = zeros8
        return carry

    lax.fori_loop(0, 12, assemble, 0)

    shrink = (OFFSETS, (-1, 0, 1), (-1, 0, 1), (0,))

    def wavefields(i, carry):
        speed = {p: cn[p][0] for p in OFFSETS}
        gen = {p: ext[p][0, i] for p in OFFSETS}
        gen_old = {p: ext[p][1, i] for p in OFFSETS}
        corr = {p: ext[p][0, 3 + i] for p in OFFSETS}
        corr_old = {p: ext[p][1, 3 + i] for p in OFFSETS}
        for n in range(STEPS):
            gen_new = advance(gen, gen_old, speed, shrink[n], lane)
            corr_new = advance(corr, corr_old, speed, shrink[n], lane)
            for p in shrink[n]:
                corr_new[p] = corr_new[p] + (cn[p][1] * weights[n]) * gen[p]
            gen_old, gen = gen, gen_new
            corr_old, corr = corr, corr_new
            snap[n, i] = gen[0][0:ROWS]
        last = corr[0][0:ROWS]
        out_corr[i, 0] = last[:, 0:DEEP]
        out_corr[i, 1] = last[:, DEEP:128]
        return carry

    lax.fori_loop(0, 3, wavefields, 0)

    def gather_sum(k, group, own_part):
        drain(k, group, 1)
        part = own_part
        for r in range(PEERS[group]):
            part = part + slots[k, r]
        total[k] = part
        return part

    gather_sum(0, "xc", chunks[me_xc])
    post(1, "y", lambda r: total.at[0], lambda r: slots.at[1, r - 1])

    def first_adjoint(ch, carry):
        speed = {p: cn[p][0] for p in OFFSETS}
        now = {p: ext[p][0, ch] for p in OFFSETS}
        old = {p: ext[p][1, ch] for p in OFFSETS}
        new = advance(now, old, speed, OFFSETS, lane)
        for p in OFFSETS:
            adj_one[ch, p + 2] = new[p]
        return carry

    lax.fori_loop(0, 6, lambda c, carry: first_adjoint(c + 6, carry), 0)
    gather_sum(1, "y", total[0])
    post(2, "z", lambda r: total.at[1], lambda r: slots.at[2, r - 1])
    ids = lax.broadcasted_iota(jnp.int32, (STATIONS, PAIRS), 0)
    first_hot[...] = jnp.where(ids == v_pairs[0:1], 1.0, 0.0).astype(BF16)
    second_hot[...] = jnp.where(ids == v_pairs[1:2], 1.0, 0.0).astype(BF16)
    rec[...] = jnp.zeros(rec.shape, F32)
    obs[...] = jnp.zeros(obs.shape, F32)
    for n in range(STEPS):
        obs[3 * n : 3 * n + 3] = v_obs[n]
    gathered[me_xc] = gather_sum(2, "z", total[1])
    post(3, "xc", lambda r: total.at[2], lambda r: gathered.at[me_xc])
    ref = gathered.at[pl.ds(0, 7)]
    pltpu.make_async_copy(ref, ref, group_sem.at[1, 3]).wait()

    for n in range(STEPS):
        for f in range(2):
            tile = gathered[2 * n + f]
            rec[f, 3 * n : 3 * n + 3, 0:128] = tile[0:3]
            rec[f, 3 * n : 3 * n + 3, 128:256] = tile[3:6]

    def thirds(v, hot, times):
        stack = jnp.concatenate(split3(v), axis=0)
        got = times(stack, hot)
        return got[0:16] + got[16:32] + got[32:48]

    first = first_hot[...]
    second = second_hot[...]
    gen_a = thirds(rec[0], first, dot)
    corr_b = thirds(rec[1], second, dot)
    misfit = gen_a * corr_b - obs[...]
    src = (thirds(misfit * corr_b, first, dot_t), thirds(misfit * gen_a, second, dot_t))

    speed = {p: cn[p][0] for p in OFFSETS}
    hot = depth_hot[0:128]
    now = {}
    old = {}
    for c in range(6):
        now[c] = {p: adj_one[6 + c, p + 2] for p in OFFSETS}
        old[c] = {p: ext[p][0, 6 + c] for p in OFFSETS}
    kernel = jnp.zeros((ROWS, 128), F32)
    halves = [split2(s) for s in src]
    for k in range(STEPS):
        later = STEPS - 1 - k
        for c in range(6):
            if k:
                new = advance(now[c], old[c], speed, shrink[k], lane)
                old[c], now[c] = now[c], new
            line = 3 * later + c % 3
            lhs = []
            for h in halves[c // 3]:
                mine = jnp.broadcast_to(h[line : line + 1].astype(F32), (ROUND, STATIONS))
                for p in shrink[k]:
                    lhs.append(
                        jnp.where(spot == row_id + (p + 2) * ROUND, mine, 0.0).astype(BF16)
                    )
            put = dot_t(jnp.concatenate(lhs, axis=0), hot)
            count = len(shrink[k])
            for j, p in enumerate(shrink[k]):
                now[c][p] = (
                    now[c][p]
                    + put[j * ROUND : (j + 1) * ROUND]
                    + put[(count + j) * ROUND : (count + j + 1) * ROUND]
                )
            if c >= 3:
                kernel = kernel + now[c][0][0:ROWS] * snap[later, c - 3]
    for c in range(6):
        last = now[c][0][0:ROWS]
        out_adj[c, 0] = last[:, 0:DEEP]
        out_adj[c, 1] = last[:, DEEP:128]
    out_kernel[0] = kernel[:, 0:DEEP]
    out_kernel[1] = kernel[:, DEEP:128]

    for copies in (cn_copies, bulk):
        for copy, da in copies:
            if da:
                pl.when(sends(da))(copy.wait_send)
            else:
                copy.wait_send()
    for k, group in enumerate(("xc", "y", "z", "xc")):
        drain(k, group, 0)


def shards(
    gen_prev,
    gen_cur,
    corr_prev,
    corr_cur,
    adj_prev,
    adj_cur,
    courant,
    noise,
    station_owner,
    station_cell,
    pairs,
    observed,
    checkpoint,
):
    anywhere = pl.BlockSpec(memory_space=pl.ANY)
    vmem = pl.BlockSpec(memory_space=pltpu.VMEM)
    ext = pltpu.VMEM((2, 12, ROUND, 128), F32)
    cn = pltpu.VMEM((2, ROUND, 128), F32)
    return pl.pallas_call(
        body,
        name="window",
        out_shape=(
            jax.ShapeDtypeStruct((3, LONG, ROWS, DEEP), F32),
            jax.ShapeDtypeStruct((6, LONG, ROWS, DEEP), F32),
            jax.ShapeDtypeStruct((LONG, ROWS, DEEP), F32),
        ),
        in_specs=[anywhere] * 12 + [pl.BlockSpec(memory_space=pltpu.SMEM)],
        out_specs=(vmem, vmem, vmem),
        scratch_shapes=[
            pltpu.VMEM((2, 12, LONG, ROWS, DEEP), F32),
            pltpu.VMEM((2, LONG, ROWS, DEEP), F32),
            pltpu.VMEM((1, STATIONS), jnp.int32),
            pltpu.VMEM((1, STATIONS), jnp.int32),
            pltpu.VMEM((2, PAIRS), jnp.int32),
            pltpu.VMEM((STEPS, 3, PAIRS), F32),
            ext,
            ext,
            ext,
            ext,
            ext,
            cn,
            cn,
            cn,
            cn,
            cn,
            pltpu.VMEM((2, 5, 2, 8, 128), F32),
            pltpu.VMEM((2, 12, 8, 128), F32),
            pltpu.VMEM((2, 3, 12, 8, 128), F32),
            pltpu.VMEM((2, 16, 128), F32),
            pltpu.VMEM((2, 2, 16, 128), F32),
            pltpu.VMEM((STEPS, 3, ROWS, 128), F32),
            pltpu.VMEM((12, 5, ROUND, 128), F32),
            pltpu.VMEM((256, STATIONS), BF16),
            pltpu.VMEM((STATIONS, PAIRS), BF16),
            pltpu.VMEM((STATIONS, PAIRS), BF16),
            pltpu.VMEM((16, PAIRS), F32),
            pltpu.VMEM((8, 8, 128), F32),
            pltpu.VMEM((3, 8, 128), F32),
            pltpu.VMEM((3, 11, 8, 128), F32),
            pltpu.VMEM((8, 8, 128), F32),
            pltpu.VMEM((2, 16, STATIONS), F32),
            pltpu.SemaphoreType.DMA((12,)),
            pltpu.SemaphoreType.DMA((2, 14)),
            pltpu.SemaphoreType.DMA((2, 14)),
            pltpu.SemaphoreType.DMA((2, 4)),
        ],
        compiler_params=pltpu.CompilerParams(
            collective_id=0, has_side_effects=True, vmem_limit_bytes=48 * 1024 * 1024
        ),
    )(
        gen_prev,
        gen_cur,
        corr_prev,
        corr_cur,
        adj_prev,
        adj_cur,
        courant,
        noise,
        station_owner.reshape(1, STATIONS),
        station_cell.reshape(1, STATIONS),
        pairs,
        observed,
        checkpoint,
    )


def solution(mesh):
    field = P(None, "lon", "lat", None)
    cells = P("lon", "lat", None)
    return jax.shard_map(
        shards,
        mesh=mesh,
        in_specs=(field,) * 6 + (cells,) * 2 + (P(),) * 5,
        out_specs=(field, field, cells),
        check_vma=False,
    )
```

profile of v0, /device:TPU:1, one launch (start us, length us, event | category | flops | bytes accessed | tf_op | source)
XLA Modules:
  0.0 69.7 jit_solution(741021011972676189)
XLA Ops:
  0.6 0.0 copy-start
  1.3 0.0 copy-start.6
  1.3 0.0 copy-start.9
  1.3 0.0 copy-start.10
  1.4 0.9 %copy.16.observed = f32[4,3,1024]{2,1,0:T(4,128)S(1)} copy(f32[4,3,1024]{2,0,1:T(4,128)} %param.24) | data formatting | bytes 98304 | tf_op args[11]
  2.2 0.0 copy-done
  2.2 0.0 copy-done.6
  2.2 0.0 copy-done.9
  2.2 0.0 copy-done.10
  2.2 0.0 copy-start.1
  2.3 0.9 %copy-done.1 = f32[6,2,16,64]{3,2,1,0:T(8,128)S(1)} copy-done((f32[6,2,16,64]{3,2,1,0:T(8,128)S(1)}, f32[6,2,16,64]{3,2,1,0:T(8,128)}, u32[]{:S(2)}) %copy-start.1) | copy-done | bytes 49176
  3.1 0.0 copy-start.2
  3.1 0.8 %copy-done.2 = f32[3,2,16,64]{3,2,1,0:T(8,128)S(1)} copy-done((f32[3,2,16,64]{3,2,1,0:T(8,128)S(1)}, f32[3,2,16,64]{3,2,1,0:T(8,128)}, u32[]{:S(2)}) %copy-start.2) | copy-done | bytes 24600
  3.9 0.0 copy-start.3
  3.9 0.8 %copy-done.3 = f32[3,2,16,64]{3,2,1,0:T(8,128)S(1)} copy-done((f32[3,2,16,64]{3,2,1,0:T(8,128)S(1)}, f32[3,2,16,64]{3,2,1,0:T(8,128)}, u32[]{:S(2)}) %copy-start.3) | copy-done | bytes 24600
  4.7 0.0 copy-start.4
  4.7 0.8 %copy-done.4 = f32[3,2,16,64]{3,2,1,0:T(8,128)S(1)} copy-done((f32[3,2,16,64]{3,2,1,0:T(8,128)S(1)}, f32[3,2,16,64]{3,2,1,0:T(8,128)}, u32[]{:S(2)}) %copy-start.4) | copy-done | bytes 24600
  5.5 0.0 copy-start.5
  5.5 0.8 %copy-done.5 = f32[3,2,16,64]{3,2,1,0:T(8,128)S(1)} copy-done((f32[3,2,16,64]{3,2,1,0:T(8,128)S(1)}, f32[3,2,16,64]{3,2,1,0:T(8,128)}, u32[]{:S(2)}) %copy-start.5) | copy-done | bytes 24600
  6.3 0.0 copy-start.7
  6.3 0.7 %copy-done.7 = f32[2,16,64]{2,1,0:T(8,128)S(1)} copy-done((f32[2,16,64]{2,1,0:T(8,128)S(1)}, f32[2,16,64]{2,1,0:T(8,128)}, u32[]{:S(2)}) %copy-start.7) | copy-done | bytes 8216
  7.1 0.0 copy-start.8
  7.1 0.7 copy-done.8
  7.8 60.1 %window.1 = (f32[3,2,16,64]{3,2,1,0:T(8,128)S(1)}, f32[6,2,16,64]{3,2,1,0:T(8,128)S(1)}, f32[2,16,64]{2,1,0:T(8,128)S(1)}) custom-call(f32[3,2,16,64]{3,2,1,0:T(8,128)S(1)} %copy-done.2, f32[3,2,16,64]{3,2,1,0:T(8,128)S(1)} %copy-done.3, f32[3,2,16,64]{3,2,1,0:T(8,128)S(1)} %copy-done.4, f32[3,2,16,64]{3,2,1,0:T(8,128)S(1)} %copy-done.5, ...), custom_call_target="tpu_custom_call" | custom-call | tf_op jit(solution)/shard_map/window/pallas_call | solution.py:576
  67.8 0.6 copy.21
  68.5 0.6 copy.22
  69.1 0.6 copy.23
Async XLA Ops:
  0.6 1.6 %copy-start = (f32[6,2,16,64]{3,2,1,0:T(8,128)S(1)}, f32[6,2,16,64]{3,2,1,0:T(8,128)}, u32[]{:S(2)}) copy-start(f32[6,2,16,64]{3,2,1,0:T(8,128)} %adj_prev.1) | copy-start | bytes 147460
  1.3 0.9 %copy-start.6 = (f32[2,16,64]{2,1,0:T(8,128)S(1)}, f32[2,16,64]{2,1,0:T(8,128)}, u32[]{:S(2)}) copy-start(f32[2,16,64]{2,1,0:T(8,128)} %courant.1) | copy-start | bytes 24580
  1.3 0.9 %copy-start.9 = (s32[256]{0:T(256)S(1)}, s32[256]{0:T(256)}, u32[]{:S(2)}) copy-start(s32[256]{0:T(256)} %param.21) | copy-start | bytes 3076
  1.3 0.9 %copy-start.10 = (s32[256]{0:T(256)S(1)}, s32[256]{0:T(256)}, u32[]{:S(2)}) copy-start(s32[256]{0:T(256)} %param.22) | copy-start | bytes 3076
  2.2 0.9 %copy-start.1 = (f32[6,2,16,64]{3,2,1,0:T(8,128)S(1)}, f32[6,2,16,64]{3,2,1,0:T(8,128)}, u32[]{:S(2)}) copy-start(f32[6,2,16,64]{3,2,1,0:T(8,128)} %adj_cur.1) | copy-start | bytes 147460
  3.1 0.8 %copy-start.2 = (f32[3,2,16,64]{3,2,1,0:T(8,128)S(1)}, f32[3,2,16,64]{3,2,1,0:T(8,128)}, u32[]{:S(2)}) copy-start(f32[3,2,16,64]{3,2,1,0:T(8,128)} %gen_prev.1) | copy-start | bytes 73732
  3.9 0.8 %copy-start.3 = (f32[3,2,16,64]{3,2,1,0:T(8,128)S(1)}, f32[3,2,16,64]{3,2,1,0:T(8,128)}, u32[]{:S(2)}) copy-start(f32[3,2,16,64]{3,2,1,0:T(8,128)} %gen_cur.1) | copy-start | bytes 73732
  4.7 0.8 %copy-start.4 = (f32[3,2,16,64]{3,2,1,0:T(8,128)S(1)}, f32[3,2,16,64]{3,2,1,0:T(8,128)}, u32[]{:S(2)}) copy-start(f32[3,2,16,64]{3,2,1,0:T(8,128)} %corr_prev.1) | copy-start | bytes 73732
  5.5 0.8 %copy-start.5 = (f32[3,2,16,64]{3,2,1,0:T(8,128)S(1)}, f32[3,2,16,64]{3,2,1,0:T(8,128)}, u32[]{:S(2)}) copy-start(f32[3,2,16,64]{3,2,1,0:T(8,128)} %corr_cur.1) | copy-start | bytes 73732
  6.3 0.7 %copy-start.7 = (f32[2,16,64]{2,1,0:T(8,128)S(1)}, f32[2,16,64]{2,1,0:T(8,128)}, u32[]{:S(2)}) copy-start(f32[2,16,64]{2,1,0:T(8,128)} %noise.1) | copy-start | bytes 24580
  7.1 0.7 copy-start.8
where the time goes:
time: 70.3 us; the launch traced here: 69.7 us
  Pallas kernels  60.1 us (85%)
  local copies, waits for them, and re-layouts  8.23 us (12%)
  between operations  1.4 us (2%)
    pallas_call x1, Pallas kernels, shards(): pl.pallas_call(body, name='window', out_shape=(jax.ShapeDtypeStruct((3, L...  60.1 us
    unnamed x26, local copies, waits for them, and re-layouts  8.23 us

commit v1 on v0

--- a/solution.py
+++ b/solution.py
@@ -116,23 +116,17 @@
     v_cell,
     v_pairs,
     v_obs,
-    e0,
-    e1,
-    e2,
-    e3,
-    e4,
+    fields,
     c0,
     c1,
     c2,
     c3,
     c4,
     cn_strip,
-    strip_out,
-    strip_in,
+    side_out,
+    side_in,
     row_out,
     row_in,
-    snap,
-    adj_one,
     depth_hot,
     first_hot,
     second_hot,
@@ -144,11 +138,10 @@
     rec,
     load_sem,
     cn_sem,
-    bulk_sem,
+    halo_sem,
     group_sem,
 ):
     lon, lat, block, inner = place()
-    ext = {-2: e0, -1: e1, 0: e2, 1: e3, 2: e4}
     cn = {-2: c0, -1: c1, 0: c2, 1: c3, 2: c4}
     loads = []
     sources = [
@@ -198,25 +191,6 @@
     loads[1].wait()
     for ch in range(2):
         c2[ch, 0:ROWS] = jnp.concatenate([st_cn[ch, 0], st_cn[ch, 1]], axis=1)
-    for k in range(2, 8):
-        loads[k].wait()
-
-    def pack(ch, carry):
-        for t in range(2):
-            wide = jnp.concatenate([st_fields[t, ch, 0], st_fields[t, ch, 1]], axis=1)
-            e2[t, ch, 0:ROWS] = wide
-        now = e2[0, ch, 0:ROWS]
-        old = e2[1, ch, 0:ROWS]
-        strip_out[0, ch] = jnp.where(sub8 < 4, now[0:8], pltpu.roll(old[0:8], 4, 0))
-        strip_out[1, ch] = jnp.where(sub8 < 4, pltpu.roll(now[8:16], 4, 0), old[8:16])
-        row_out[0, pl.ds(ch, 1)] = now[0:1]
-        row_out[1, pl.ds(ch, 1)] = now[ROWS - 1 : ROWS]
-        return carry
-
-    lax.fori_loop(0, 12, pack, 0)
-    for k in range(8, 12):
-        loads[k].wait()
-
     pl.semaphore_wait(barrier, greeted)
 
     has_low = lat > 0
@@ -260,46 +234,6 @@
                     da,
                 )
             )
-    bulk = []
-    for dl in (-1, 1, -2, 2):
-        bulk.append(
-            (
-                remote(
-                    e2.at[:, :, pl.ds(0, ROWS)],
-                    ext[-dl].at[:, :, pl.ds(0, ROWS)],
-                    bulk_sem,
-                    len(bulk),
-                    dl,
-                    0,
-                ),
-                0,
-            )
-        )
-    for dl in (0, -1, 1):
-        for da in (-1, 1):
-            d = 0 if da < 0 else 1
-            bulk.append(
-                (
-                    remote(strip_out.at[d], strip_in.at[d, 1 - dl], bulk_sem, len(bulk), dl, da),
-                    da,
-                )
-            )
-    for dl in (-2, 2):
-        for da in (-1, 1):
-            d = 0 if da < 0 else 1
-            bulk.append(
-                (
-                    remote(
-                        row_out.at[d],
-                        row_in.at[d, 0 if dl > 0 else 1],
-                        bulk_sem,
-                        len(bulk),
-                        dl,
-                        da,
-                    ),
-                    da,
-                )
-            )
 
     def sends(da):
         return has_low if da < 0 else has_high
@@ -307,7 +241,7 @@
     def receives(da):
         return has_high if da < 0 else has_low
 
-    for copies in (cn_copies, bulk):
+    def go(copies):
         for copy, da in copies:
             if da:
                 pl.when(sends(da))(copy.start)
@@ -320,6 +254,54 @@
                 pl.when(receives(da))(copy.wait_recv)
             else:
                 copy.wait_recv()
+
+    go(cn_copies)
+
+    for k in range(2, 8):
+        loads[k].wait()
+
+    def pack(ch, carry):
+        for t in range(2):
+            wide = jnp.concatenate([st_fields[t, ch, 0], st_fields[t, ch, 1]], axis=1)
+            fields[1 - t, ch] = wide
+        return carry
+
+    lax.fori_loop(0, 12, pack, 0)
+    lane16 = lane[0:ROWS]
+    row16 = lax.broadcasted_iota(jnp.int32, (ROWS, 128), 0)
+
+    def halo(n):
+        copies = []
+        for d, dl in enumerate((-1, 1)):
+            copies.append(
+                (remote(side_out.at[n, d], side_in.at[n, d], halo_sem.at[n], len(copies), dl, 0), 0)
+            )
+        for d, da in enumerate((-1, 1)):
+            copies.append(
+                (remote(row_out.at[n, d], row_in.at[n, d], halo_sem.at[n], len(copies), 0, da), da)
+            )
+        return copies
+
+    def send_halo(n):
+        def fill(c, carry):
+            one = fields[n + 1, c]
+            two = fields[n + 1, c + 6]
+            turned = pltpu.roll(two, DEEP, 1)
+            side_out[n, 0, c] = jnp.where(lane16 < DEEP, one, turned)
+            side_out[n, 1, c] = jnp.where(lane16 < DEEP, turned, one)
+            for half, x in ((0, one), (6, two)):
+                row_out[n, 0, pl.ds(c + half, 1)] = x[0:1]
+                row_out[n, 1, pl.ds(c + half, 1)] = x[ROWS - 1 : ROWS]
+            return carry
+
+        lax.fori_loop(0, 6, fill, 0)
+        copies = halo(n)
+        go(copies)
+        return copies
+
+    halos = [send_halo(0)]
+    for k in range(8, 12):
+        loads[k].wait()
 
     own = v_owner[...]
     where_in = v_cell[...]
@@ -341,6 +323,17 @@
     phase = checkpoint[0].astype(F32)
     weights = [jnp.cos(jnp.full((ROUND, 128), OMEGA * (phase + n), F32)) for n in range(STEPS)]
 
+    ids = lax.broadcasted_iota(jnp.int32, (STATIONS, PAIRS), 0)
+    first_hot[...] = jnp.where(ids == v_pairs[0:1], 1.0, 0.0).astype(BF16)
+    second_hot[...] = jnp.where(ids == v_pairs[1:2], 1.0, 0.0).astype(BF16)
+    rec[...] = jnp.zeros(rec.shape, F32)
+    obs[...] = jnp.zeros(obs.shape, F32)
+    for n in range(STEPS):
+        for i in range(3):
+            obs[3 * n + i : 3 * n + i + 1] = v_obs[i, n : n + 1]
+    for j in range(8):
+        chunks[j, 6:8] = jnp.zeros((2, 128), F32)
+
     take(cn_copies)
     for p in OFFSETS:
         for ch in range(2):
@@ -353,7 +346,7 @@
         pad = jnp.zeros((8, 128), F32)
 
         def own_cells(t, ch):
-            return jnp.concatenate([e2[t, ch, 0:ROWS], pad], axis=0)
+            return jnp.concatenate([fields[1 - t, ch], pad], axis=0)
 
         speed = {p: cn[p][0] for p in OFFSETS}
         gen = {0: own_cells(0, i)}
@@ -383,8 +376,6 @@
                 chunks[2 * n + f, pl.ds(3 + i, 1)] = line[:, 128:256]
         return carry
 
-    for j in range(8):
-        chunks[j, 6:8] = jnp.zeros((2, 128), F32)
     lax.fori_loop(0, 3, responses, 0)
 
     me_xc = block % 4 * 2 + inner % 2
@@ -409,47 +400,43 @@
 
     post(0, "xc", lambda r: chunks.at[(me_xc + r) % 8], lambda r: slots.at[0, r - 1])
 
-    take(bulk)
-
-    def assemble(ch, carry):
-        for p in STRIPS:
-            above = jnp.where(has_high, strip_in[0, p + 1, ch], zeros8)
-            below = jnp.where(has_low, strip_in[1, p + 1, ch], zeros8)
-            ext[p][0, ch, ROWS:ROUND] = jnp.where(sub8 < 4, above, pltpu.roll(below, 4, 0))
-            ext[p][1, ch, ROWS:ROUND] = jnp.where(sub8 < 4, pltpu.roll(above, 4, 0), below)
-        for k, p in enumerate((-2, 2)):
-            above = jnp.where(has_high, row_in[0, k, pl.ds(ch, 1)], 0.0)
-            below = jnp.where(has_low, row_in[1, k, pl.ds(ch, 1)], 0.0)
-            ext[p][0, ch, ROWS:ROUND] = jnp.where(
-                sub8 == 0, above, jnp.where(sub8 == 7, below, 0.0)
-            )
-            ext[p][1, ch, ROWS:ROUND] = zeros8
-        return carry
-
-    lax.fori_loop(0, 12, assemble, 0)
+    def step(n):
+        take(halos[n])
+        speed = c2[0, 0:ROWS]
+
+        def one(c, twice):
+            x = fields[n + 1, c]
+            low = side_in[n, 1, c - 6 if twice else c]
+            high = side_in[n, 0, c - 6 if twice else c]
+            if twice:
+                along_lon = pltpu.roll(x, DEEP, 1) + jnp.where(lane16 < DEEP, low, high)
+            else:
+                along_lon = pltpu.roll(x + jnp.where(lane16 < DEEP, high, low), DEEP, 1)
+            deeper = jnp.where(lane16 % DEEP == 0, 0.0, pltpu.roll(x, 1, 1))
+            higher = jnp.where(lane16 % DEEP == DEEP - 1, 0.0, pltpu.roll(x, 127, 1))
+            below = jnp.where(has_low, row_in[n, 1, pl.ds(c, 1)], 0.0)
+            above = jnp.where(has_high, row_in[n, 0, pl.ds(c, 1)], 0.0)
+            north = jnp.where(row16 == 0, below, pltpu.roll(x, 1, 0))
+            south = jnp.where(row16 == ROWS - 1, above, pltpu.roll(x, ROWS - 1, 0))
+            around = along_lon + (north + south + deeper + higher) - 6.0 * x
+            return 2.0 * x - fields[n, c] + speed * around
+
+        def component(i, carry):
+            fields[n + 2, i] = one(i, False)
+            fields[n + 2, 3 + i] = one(3 + i, False) + (
+                c2[1, 0:ROWS] * weights[n][0:ROWS]
+            ) * fields[n + 1, i]
+            fields[n + 2, 6 + i] = one(6 + i, True)
+            fields[n + 2, 9 + i] = one(9 + i, True)
+            return carry
+
+        lax.fori_loop(0, 3, component, 0)
+        if n + 1 < STEPS:
+            halos.append(send_halo(n + 1))
+
+    step(0)
 
     shrink = (OFFSETS, (-1, 0, 1), (-1, 0, 1), (0,))
-
-    def wavefields(i, carry):
-        speed = {p: cn[p][0] for p in OFFSETS}
-        gen = {p: ext[p][0, i] for p in OFFSETS}
-        gen_old = {p: ext[p][1, i] for p in OFFSETS}
-        corr = {p: ext[p][0, 3 + i] for p in OFFSETS}
-        corr_old = {p: ext[p][1, 3 + i] for p in OFFSETS}
-        for n in range(STEPS):
-            gen_new = advance(gen, gen_old, speed, shrink[n], lane)
-            corr_new = advance(corr, corr_old, speed, shrink[n], lane)
-            for p in shrink[n]:
-                corr_new[p] = corr_new[p] + (cn[p][1] * weights[n]) * gen[p]
-            gen_old, gen = gen, gen_new
-            corr_old, corr = corr, corr_new
-            snap[n, i] = gen[0][0:ROWS]
-        last = corr[0][0:ROWS]
-        out_corr[i, 0] = last[:, 0:DEEP]
-        out_corr[i, 1] = last[:, DEEP:128]
-        return carry
-
-    lax.fori_loop(0, 3, wavefields, 0)
 
     def gather_sum(k, group, own_part):
         drain(k, group, 1)
@@ -462,25 +449,10 @@
     gather_sum(0, "xc", chunks[me_xc])
     post(1, "y", lambda r: total.at[0], lambda r: slots.at[1, r - 1])
 
-    def first_adjoint(ch, carry):
-        speed = {p: cn[p][0] for p in OFFSETS}
-        now = {p: ext[p][0, ch] for p in OFFSETS}
-        old = {p: ext[p][1, ch] for p in OFFSETS}
-        new = advance(now, old, speed, OFFSETS, lane)
-        for p in OFFSETS:
-            adj_one[ch, p + 2] = new[p]
-        return carry
-
-    lax.fori_loop(0, 6, lambda c, carry: first_adjoint(c + 6, carry), 0)
+    step(1)
     gather_sum(1, "y", total[0])
     post(2, "z", lambda r: total.at[1], lambda r: slots.at[2, r - 1])
-    ids = lax.broadcasted_iota(jnp.int32, (STATIONS, PAIRS), 0)
-    first_hot[...] = jnp.where(ids == v_pairs[0:1], 1.0, 0.0).astype(BF16)
-    second_hot[...] = jnp.where(ids == v_pairs[1:2], 1.0, 0.0).astype(BF16)
-    rec[...] = jnp.zeros(rec.shape, F32)
-    obs[...] = jnp.zeros(obs.shape, F32)
-    for n in range(STEPS):
-        obs[3 * n : 3 * n + 3] = v_obs[n]
+    step(2)
     gathered[me_xc] = gather_sum(2, "z", total[1])
     post(3, "xc", lambda r: total.at[2], lambda r: gathered.at[me_xc])
     ref = gathered.at[pl.ds(0, 7)]
@@ -506,19 +478,15 @@
 
     speed = {p: cn[p][0] for p in OFFSETS}
     hot = depth_hot[0:128]
-    now = {}
-    old = {}
-    for c in range(6):
-        now[c] = {p: adj_one[6 + c, p + 2] for p in OFFSETS}
-        old[c] = {p: ext[p][0, 6 + c] for p in OFFSETS}
-    kernel = jnp.zeros((ROWS, 128), F32)
-    halves = [split2(s) for s in src]
+    now = [{} for c in range(6)]
+    old = [{} for c in range(6)]
+    added = []
+    halves = [split2(v) for v in src]
     for k in range(STEPS):
         later = STEPS - 1 - k
         for c in range(6):
-            if k:
-                new = advance(now[c], old[c], speed, shrink[k], lane)
-                old[c], now[c] = now[c], new
+            new = advance(now[c], old[c], speed, shrink[k], lane) if k else {}
+            old[c] = now[c]
             line = 3 * later + c % 3
             lhs = []
             for h in halves[c // 3]:
@@ -530,21 +498,31 @@
             put = dot_t(jnp.concatenate(lhs, axis=0), hot)
             count = len(shrink[k])
             for j, p in enumerate(shrink[k]):
-                now[c][p] = (
-                    now[c][p]
-                    + put[j * ROUND : (j + 1) * ROUND]
+                both = (
+                    put[j * ROUND : (j + 1) * ROUND]
                     + put[(count + j) * ROUND : (count + j + 1) * ROUND]
                 )
-            if c >= 3:
-                kernel = kernel + now[c][0][0:ROWS] * snap[later, c - 3]
+                new[p] = new[p] + both if k else both
+            now[c] = new
+        added.append([now[c][0][0:ROWS] for c in range(6)])
+
+    step(3)
+    kernel = jnp.zeros((ROWS, 128), F32)
+    for k in range(STEPS):
+        for c in range(3):
+            kernel = kernel + (fields[k + 2, 9 + c] + added[k][3 + c]) * fields[STEPS + 1 - k, c]
+    for c in range(3):
+        last = fields[STEPS + 1, 3 + c]
+        out_corr[c, 0] = last[:, 0:DEEP]
+        out_corr[c, 1] = last[:, DEEP:128]
     for c in range(6):
-        last = now[c][0][0:ROWS]
+        last = fields[STEPS + 1, 6 + c] + added[STEPS - 1][c]
         out_adj[c, 0] = last[:, 0:DEEP]
         out_adj[c, 1] = last[:, DEEP:128]
     out_kernel[0] = kernel[:, 0:DEEP]
     out_kernel[1] = kernel[:, DEEP:128]
 
-    for copies in (cn_copies, bulk):
+    for copies in [cn_copies] + halos:
         for copy, da in copies:
             if da:
                 pl.when(sends(da))(copy.wait_send)
@@ -569,9 +547,8 @@
     observed,
     checkpoint,
 ):
-    anywhere = pl.BlockSpec(memory_space=pl.ANY)
+    anywhere = pl.BlockSpec(memory_space=pltpu.HBM)
     vmem = pl.BlockSpec(memory_space=pltpu.VMEM)
-    ext = pltpu.VMEM((2, 12, ROUND, 128), F32)
     cn = pltpu.VMEM((2, ROUND, 128), F32)
     return pl.pallas_call(
         body,
@@ -589,24 +566,18 @@
             pltpu.VMEM((1, STATIONS), jnp.int32),
             pltpu.VMEM((1, STATIONS), jnp.int32),
             pltpu.VMEM((2, PAIRS), jnp.int32),
-            pltpu.VMEM((STEPS, 3, PAIRS), F32),
-            ext,
-            ext,
-            ext,
-            ext,
-            ext,
+            pltpu.VMEM((3, STEPS, PAIRS), F32),
+            pltpu.VMEM((STEPS + 2, 12, ROWS, 128), F32),
             cn,
             cn,
             cn,
             cn,
             cn,
             pltpu.VMEM((2, 5, 2, 8, 128), F32),
-            pltpu.VMEM((2, 12, 8, 128), F32),
-            pltpu.VMEM((2, 3, 12, 8, 128), F32),
-            pltpu.VMEM((2, 16, 128), F32),
-            pltpu.VMEM((2, 2, 16, 128), F32),
-            pltpu.VMEM((STEPS, 3, ROWS, 128), F32),
-            pltpu.VMEM((12, 5, ROUND, 128), F32),
+            pltpu.VMEM((STEPS, 2, 6, ROWS, 128), F32),
+            pltpu.VMEM((STEPS, 2, 6, ROWS, 128), F32),
+            pltpu.VMEM((STEPS, 2, 16, 128), F32),
+            pltpu.VMEM((STEPS, 2, 16, 128), F32),
             pltpu.VMEM((256, STATIONS), BF16),
             pltpu.VMEM((STATIONS, PAIRS), BF16),
             pltpu.VMEM((STATIONS, PAIRS), BF16),
@@ -618,11 +589,11 @@
             pltpu.VMEM((2, 16, STATIONS), F32),
             pltpu.SemaphoreType.DMA((12,)),
             pltpu.SemaphoreType.DMA((2, 14)),
-            pltpu.SemaphoreType.DMA((2, 14)),
+            pltpu.SemaphoreType.DMA((STEPS, 2, 4)),
             pltpu.SemaphoreType.DMA((2, 4)),
         ],
         compiler_params=pltpu.CompilerParams(
-            collective_id=0, has_side_effects=True, vmem_limit_bytes=48 * 1024 * 1024
+            collective_id=0, has_side_effects=True, vmem_limit_bytes=56 * 1024 * 1024
         ),
     )(
         gen_prev,
@@ -636,7 +607,7 @@
         station_owner.reshape(1, STATIONS),
         station_cell.reshape(1, STATIONS),
         pairs,
-        observed,
+        jnp.transpose(observed, (1, 0, 2)),
         checkpoint,
     )
 

time: 70.3 us -> 57.6 us (0.82)
  the two profiles are of different devices: /device:TPU:1 before, /device:TPU:8 now
where the time goes in v1:
time: 57.6 us; the launch traced here: 57.4 us
  Pallas kernels  53.3 us (93%)
  local copies, waits for them, and re-layouts  2.78 us (5%)
  between operations  1.3 us (2%)
    pallas_call x1, Pallas kernels, shards(): pl.pallas_call(body, name='window', out_shape=(jax.ShapeDtypeStruct((3, L...  53.3 us
    unnamed x7, local copies, waits for them, and re-layouts  2.78 us

profile of v1, /device:TPU:8, one launch (start us, length us, event | category | flops | bytes accessed | tf_op | source)
XLA Modules:
  0.0 57.4 jit_solution(11979752818147765312)
XLA Ops:
  1.3 53.3 %window.1 = (f32[3,2,16,64]{3,2,1,0:T(8,128)}, f32[6,2,16,64]{3,2,1,0:T(8,128)}, f32[2,16,64]{2,1,0:T(8,128)}) custom-call(f32[3,2,16,64]{3,2,1,0:T(8,128)} %gen_prev.1, f32[3,2,16,64]{3,2,1,0:T(8,128)} %gen_cur.1, f32[3,2,16,64]{3,2,1,0:T(8,128)} %corr_prev.1, f32[3,2,16,64]{3,2,1,0:T(8,128)} %corr_cur.1, f32[6,2,16,64]{3,2,1,0:T(8,128)} %adj_prev.1, ...), custom_call_target="tpu_custom_call" | custom-call | tf_op jit(solution)/shard_map/window/pallas_call | solution.py:553
  54.6 0.0 copy-start
  54.6 1.5 %copy.20 = f32[3,2,16,64]{3,2,1,0:T(8,128)} copy(f32[3,2,16,64]{3,2,1,0:T(8,128)} %get-tuple-element.6) | data formatting | bytes 49152
  56.1 0.0 copy-done
  56.1 0.0 copy-start.1
  56.1 0.6 %copy.21 = f32[6,2,16,64]{3,2,1,0:T(8,128)} copy(f32[6,2,16,64]{3,2,1,0:T(8,128)S(1)} %copy-done) | data formatting | bytes 98304
  56.7 0.1 copy-done.1
  56.8 0.6 %copy.22 = f32[2,16,64]{2,1,0:T(8,128)} copy(f32[2,16,64]{2,1,0:T(8,128)S(1)} %copy-done.1) | data formatting | bytes 16384
Async XLA Ops:
  54.6 1.5 %copy-start = (f32[6,2,16,64]{3,2,1,0:T(8,128)S(1)}, f32[6,2,16,64]{3,2,1,0:T(8,128)}, u32[]{:S(2)}) copy-start(f32[6,2,16,64]{3,2,1,0:T(8,128)} %get-tuple-element.7) | copy-start | bytes 147460
  56.1 0.7 %copy-start.1 = (f32[2,16,64]{2,1,0:T(8,128)S(1)}, f32[2,16,64]{2,1,0:T(8,128)}, u32[]{:S(2)}) copy-start(f32[2,16,64]{2,1,0:T(8,128)} %get-tuple-element.8) | copy-start | bytes 24580

commit v2 on v1

--- a/solution.py
+++ b/solution.py
@@ -127,6 +127,7 @@
     side_in,
     row_out,
     row_in,
+    corner_in,
     depth_hot,
     first_hot,
     second_hot,
@@ -260,42 +261,64 @@
     for k in range(2, 8):
         loads[k].wait()
 
-    def pack(ch, carry):
+    for ch in range(12):
         for t in range(2):
             wide = jnp.concatenate([st_fields[t, ch, 0], st_fields[t, ch, 1]], axis=1)
             fields[1 - t, ch] = wide
-        return carry
-
-    lax.fori_loop(0, 12, pack, 0)
     lane16 = lane[0:ROWS]
     row16 = lax.broadcasted_iota(jnp.int32, (ROWS, 128), 0)
 
-    def halo(n):
+    def halo(h):
         copies = []
         for d, dl in enumerate((-1, 1)):
             copies.append(
-                (remote(side_out.at[n, d], side_in.at[n, d], halo_sem.at[n], len(copies), dl, 0), 0)
+                (remote(side_out.at[h, d], side_in.at[h, d], halo_sem.at[h], len(copies), dl, 0), 0)
             )
         for d, da in enumerate((-1, 1)):
             copies.append(
-                (remote(row_out.at[n, d], row_in.at[n, d], halo_sem.at[n], len(copies), 0, da), da)
+                (remote(row_out.at[h, d], row_in.at[h, d], halo_sem.at[h], len(copies), 0, da), da)
             )
+        for d, da in enumerate((-1, 1)):
+            for e, dl in enumerate((-1, 1)):
+                copies.append(
+                    (
+                        remote(
+                            row_out.at[h, d, 0],
+                            corner_in.at[h, d, e],
+                            halo_sem.at[h],
+                            len(copies),
+                            dl,
+                            da,
+                        ),
+                        da,
+                    )
+                )
         return copies
 
-    def send_halo(n):
-        def fill(c, carry):
-            one = fields[n + 1, c]
-            two = fields[n + 1, c + 6]
-            turned = pltpu.roll(two, DEEP, 1)
-            side_out[n, 0, c] = jnp.where(lane16 < DEEP, one, turned)
-            side_out[n, 1, c] = jnp.where(lane16 < DEEP, turned, one)
-            for half, x in ((0, one), (6, two)):
-                row_out[n, 0, pl.ds(c + half, 1)] = x[0:1]
-                row_out[n, 1, pl.ds(c + half, 1)] = x[ROWS - 1 : ROWS]
-            return carry
-
-        lax.fori_loop(0, 6, fill, 0)
-        copies = halo(n)
+    def turn(x):
+        return pltpu.roll(x, DEEP, 1)
+
+    def send_halo(h):
+        n = 2 * h + 1
+        for c in range(6):
+            one, two = fields[n, c], fields[n, c + 6]
+            one_t, two_t = turn(one), turn(two)
+            side_out[h, 0, 0, c] = jnp.where(lane16 < DEEP, one, two_t)
+            side_out[h, 1, 0, c] = jnp.where(lane16 < DEEP, two_t, one)
+            side_out[h, 0, 1, c] = jnp.where(lane16 < DEEP, one_t, two)
+            side_out[h, 1, 1, c] = jnp.where(lane16 < DEEP, two, one_t)
+            one, two_t = fields[n - 1, c], turn(fields[n - 1, c + 6])
+            side_out[h, 0, 2, c] = jnp.where(lane16 < DEEP, one, two_t)
+            side_out[h, 1, 2, c] = jnp.where(lane16 < DEEP, two_t, one)
+        for c in range(12):
+            now, before = fields[n, c], fields[n - 1, c]
+            row_out[h, 0, 0, c : c + 1] = now[0:1]
+            row_out[h, 0, 1, c : c + 1] = now[1:2]
+            row_out[h, 0, 2, c : c + 1] = before[0:1]
+            row_out[h, 1, 0, c : c + 1] = now[ROWS - 1 : ROWS]
+            row_out[h, 1, 1, c : c + 1] = now[ROWS - 2 : ROWS - 1]
+            row_out[h, 1, 2, c : c + 1] = before[ROWS - 1 : ROWS]
+        copies = halo(h)
         go(copies)
         return copies
 
@@ -342,7 +365,7 @@
             cn[p][ch, ROWS:ROUND] = jnp.where(sub8 < 4, above, below)
     reach = ((-1, 0, 1), (-1, 0, 1), OFFSETS, OFFSETS)
 
-    def responses(i, carry):
+    def responses(i):
         pad = jnp.zeros((8, 128), F32)
 
         def own_cells(t, ch):
@@ -372,11 +395,11 @@
                         spot == row_id + (p + 2) * ROUND, picked[at : at + ROUND], 0.0
                     )
                 line = jnp.sum(summed, axis=0, keepdims=True)
-                chunks[2 * n + f, pl.ds(i, 1)] = line[:, 0:128]
-                chunks[2 * n + f, pl.ds(3 + i, 1)] = line[:, 128:256]
-        return carry
-
-    lax.fori_loop(0, 3, responses, 0)
+                chunks[2 * n + f, i : i + 1] = line[:, 0:128]
+                chunks[2 * n + f, 3 + i : 4 + i] = line[:, 128:256]
+
+    for i in range(3):
+        responses(i)
 
     me_xc = block % 4 * 2 + inner % 2
 
@@ -400,41 +423,88 @@
 
     post(0, "xc", lambda r: chunks.at[(me_xc + r) % 8], lambda r: slots.at[0, r - 1])
 
-    def step(n):
-        take(halos[n])
+    def depth_sum(x, lanes):
+        deeper = jnp.where(lanes % DEEP == 0, 0.0, pltpu.roll(x, 1, 1))
+        higher = jnp.where(lanes % DEEP == DEEP - 1, 0.0, pltpu.roll(x, 127, 1))
+        return deeper + higher
+
+    def lat_sum(x, below, above):
+        north = jnp.where(row16 == 0, below, pltpu.roll(x, 1, 0))
+        south = jnp.where(row16 == ROWS - 1, above, pltpu.roll(x, ROWS - 1, 0))
+        return north + south
+
+    def step(n, sides, rows):
         speed = c2[0, 0:ROWS]
-
-        def one(c, twice):
+        noisy = c2[1, 0:ROWS] * weights[n][0:ROWS]
+        for c in range(12):
             x = fields[n + 1, c]
-            low = side_in[n, 1, c - 6 if twice else c]
-            high = side_in[n, 0, c - 6 if twice else c]
-            if twice:
-                along_lon = pltpu.roll(x, DEEP, 1) + jnp.where(lane16 < DEEP, low, high)
+            low, high = sides[0][c % 6], sides[1][c % 6]
+            if c < 6:
+                along_lon = turn(x + jnp.where(lane16 < DEEP, high, low))
             else:
-                along_lon = pltpu.roll(x + jnp.where(lane16 < DEEP, high, low), DEEP, 1)
-            deeper = jnp.where(lane16 % DEEP == 0, 0.0, pltpu.roll(x, 1, 1))
-            higher = jnp.where(lane16 % DEEP == DEEP - 1, 0.0, pltpu.roll(x, 127, 1))
-            below = jnp.where(has_low, row_in[n, 1, pl.ds(c, 1)], 0.0)
-            above = jnp.where(has_high, row_in[n, 0, pl.ds(c, 1)], 0.0)
-            north = jnp.where(row16 == 0, below, pltpu.roll(x, 1, 0))
-            south = jnp.where(row16 == ROWS - 1, above, pltpu.roll(x, ROWS - 1, 0))
-            around = along_lon + (north + south + deeper + higher) - 6.0 * x
-            return 2.0 * x - fields[n, c] + speed * around
-
-        def component(i, carry):
-            fields[n + 2, i] = one(i, False)
-            fields[n + 2, 3 + i] = one(3 + i, False) + (
-                c2[1, 0:ROWS] * weights[n][0:ROWS]
-            ) * fields[n + 1, i]
-            fields[n + 2, 6 + i] = one(6 + i, True)
-            fields[n + 2, 9 + i] = one(9 + i, True)
-            return carry
-
-        lax.fori_loop(0, 3, component, 0)
-        if n + 1 < STEPS:
-            halos.append(send_halo(n + 1))
-
-    step(0)
+                along_lon = turn(x) + jnp.where(lane16 < DEEP, low, high)
+            near = lat_sum(x, rows[0][c : c + 1], rows[1][c : c + 1])
+            around = along_lon + (near + depth_sum(x, lane16)) - 6.0 * x
+            new = 2.0 * x - fields[n, c] + speed * around
+            if 3 <= c < 6:
+                new = new + noisy * fields[n + 1, c - 3]
+            fields[n + 2, c] = new
+
+    def layer(h):
+        n = 2 * h
+        arrived = (has_low, has_high)
+        row = [
+            [jnp.where(arrived[d], row_in[h, 1 - d, j], 0.0) for j in range(3)] for d in range(2)
+        ]
+        corner = [
+            [jnp.where(arrived[d], corner_in[h, 1 - d, 1 - e], 0.0) for e in range(2)]
+            for d in range(2)
+        ]
+        sides_now = [[side_in[h, 1 - e, 0, c] for c in range(6)] for e in range(2)]
+        sides_new = []
+        for e in range(2):
+            own_half = lane16 >= DEEP if e == 0 else lane16 < DEEP
+            cells = cn[-1 if e == 0 else 1]
+            speed = cells[0, 0:ROWS]
+            speed = jnp.where(own_half, speed, turn(speed))
+            noisy = jnp.where(own_half, cells[1, 0:ROWS] * weights[n][0:ROWS], 0.0)
+            ends = [
+                jnp.where(own_half, corner[d][e], turn(pltpu.roll(corner[d][e], 10, 0)))
+                for d in range(2)
+            ]
+            new = []
+            for c in range(6):
+                x = sides_now[e][c]
+                along_lon = side_in[h, 1 - e, 1, c] + side_out[h, 1 - e, 1, c]
+                near = lat_sum(x, ends[0][c : c + 1], ends[1][c : c + 1])
+                around = along_lon + (near + depth_sum(x, lane16)) - 6.0 * x
+                v = 2.0 * x - side_in[h, 1 - e, 2, c] + speed * around
+                if c >= 3:
+                    v = v + noisy * sides_now[e][c - 3]
+                new.append(v)
+            sides_new.append(new)
+        rows_now = [row[d][0] for d in range(2)]
+        rows_new = []
+        for d in range(2):
+            at = ROUND - 1 if d == 0 else ROWS
+            x = rows_now[d]
+            sides = jnp.where(lane16 < DEEP, corner[d][1], corner[d][0])
+            own = row_out[h, d, 0]
+            around = turn(x + sides) + (own + row[d][1] + depth_sum(x, lane16)) - 6.0 * x
+            v = 2.0 * x - row[d][2] + c2[0, at : at + 1] * around
+            moved = jnp.where((row16 >= 3) & (row16 < 6), pltpu.roll(x, 3, 0), 0.0)
+            v = v + (c2[1, at : at + 1] * weights[n][0:1]) * moved
+            rows_new.append(v)
+        return (sides_now, rows_now), (sides_new, rows_new)
+
+    def two_steps(h):
+        take(halos[h])
+        now, new = layer(h)
+        step(2 * h, *now)
+        step(2 * h + 1, *new)
+
+    two_steps(0)
+    halos.append(send_halo(1))
 
     shrink = (OFFSETS, (-1, 0, 1), (-1, 0, 1), (0,))
 
@@ -449,10 +519,9 @@
     gather_sum(0, "xc", chunks[me_xc])
     post(1, "y", lambda r: total.at[0], lambda r: slots.at[1, r - 1])
 
-    step(1)
     gather_sum(1, "y", total[0])
     post(2, "z", lambda r: total.at[1], lambda r: slots.at[2, r - 1])
-    step(2)
+    two_steps(1)
     gathered[me_xc] = gather_sum(2, "z", total[1])
     post(3, "xc", lambda r: total.at[2], lambda r: gathered.at[me_xc])
     ref = gathered.at[pl.ds(0, 7)]
@@ -506,7 +575,6 @@
             now[c] = new
         added.append([now[c][0][0:ROWS] for c in range(6)])
 
-    step(3)
     kernel = jnp.zeros((ROWS, 128), F32)
     for k in range(STEPS):
         for c in range(3):
@@ -574,10 +642,11 @@
             cn,
             cn,
             pltpu.VMEM((2, 5, 2, 8, 128), F32),
-            pltpu.VMEM((STEPS, 2, 6, ROWS, 128), F32),
-            pltpu.VMEM((STEPS, 2, 6, ROWS, 128), F32),
-            pltpu.VMEM((STEPS, 2, 16, 128), F32),
-            pltpu.VMEM((STEPS, 2, 16, 128), F32),
+            pltpu.VMEM((2, 2, 3, 6, ROWS, 128), F32),
+            pltpu.VMEM((2, 2, 3, 6, ROWS, 128), F32),
+            pltpu.VMEM((2, 2, 3, 16, 128), F32),
+            pltpu.VMEM((2, 2, 3, 16, 128), F32),
+            pltpu.VMEM((2, 2, 2, 16, 128), F32),
             pltpu.VMEM((256, STATIONS), BF16),
             pltpu.VMEM((STATIONS, PAIRS), BF16),
             pltpu.VMEM((STATIONS, PAIRS), BF16),
@@ -589,7 +658,7 @@
             pltpu.VMEM((2, 16, STATIONS), F32),
             pltpu.SemaphoreType.DMA((12,)),
             pltpu.SemaphoreType.DMA((2, 14)),
-            pltpu.SemaphoreType.DMA((STEPS, 2, 4)),
+            pltpu.SemaphoreType.DMA((2, 2, 8)),
             pltpu.SemaphoreType.DMA((2, 4)),
         ],
         compiler_params=pltpu.CompilerParams(

time: 57.6 us -> 53.3 us (0.925)
  the two profiles are of different devices: /device:TPU:8 before, /device:TPU:1 now
where the time goes in v2:
time: 53.3 us; the launch traced here: 53.1 us
  Pallas kernels  49 us (92%)
  local copies, waits for them, and re-layouts  2.78 us (5%)
  between operations  1.3 us (2%)
    pallas_call x1, Pallas kernels, shards(): pl.pallas_call(body, name='window', out_shape=(jax.ShapeDtypeStruct((3, L...  49 us
    unnamed x7, local copies, waits for them, and re-layouts  2.78 us

profile of v2, /device:TPU:1, one launch (start us, length us, event | category | flops | bytes accessed | tf_op | source)
XLA Modules:
  0.0 53.1 jit_solution(4238773437866353957)
XLA Ops:
  1.3 49.0 %window.1 = (f32[3,2,16,64]{3,2,1,0:T(8,128)}, f32[6,2,16,64]{3,2,1,0:T(8,128)}, f32[2,16,64]{2,1,0:T(8,128)}) custom-call(f32[3,2,16,64]{3,2,1,0:T(8,128)} %gen_prev.1, f32[3,2,16,64]{3,2,1,0:T(8,128)} %gen_cur.1, f32[3,2,16,64]{3,2,1,0:T(8,128)} %corr_prev.1, f32[3,2,16,64]{3,2,1,0:T(8,128)} %corr_cur.1, f32[6,2,16,64]{3,2,1,0:T(8,128)} %adj_prev.1, ...), custom_call_target="tpu_custom_call" | custom-call | tf_op jit(solution)/shard_map/window/pallas_call | solution.py:621
  50.3 0.0 copy-start
  50.3 1.5 %copy.20 = f32[3,2,16,64]{3,2,1,0:T(8,128)} copy(f32[3,2,16,64]{3,2,1,0:T(8,128)} %get-tuple-element.6) | data formatting | bytes 49152
  51.8 0.0 copy-done
  51.8 0.0 copy-start.1
  51.8 0.6 %copy.21 = f32[6,2,16,64]{3,2,1,0:T(8,128)} copy(f32[6,2,16,64]{3,2,1,0:T(8,128)S(1)} %copy-done) | data formatting | bytes 98304
  52.4 0.1 copy-done.1
  52.5 0.6 %copy.22 = f32[2,16,64]{2,1,0:T(8,128)} copy(f32[2,16,64]{2,1,0:T(8,128)S(1)} %copy-done.1) | data formatting | bytes 16384
Async XLA Ops:
  50.3 1.5 %copy-start = (f32[6,2,16,64]{3,2,1,0:T(8,128)S(1)}, f32[6,2,16,64]{3,2,1,0:T(8,128)}, u32[]{:S(2)}) copy-start(f32[6,2,16,64]{3,2,1,0:T(8,128)} %get-tuple-element.7) | copy-start | bytes 147460
  51.8 0.7 %copy-start.1 = (f32[2,16,64]{2,1,0:T(8,128)S(1)}, f32[2,16,64]{2,1,0:T(8,128)}, u32[]{:S(2)}) copy-start(f32[2,16,64]{2,1,0:T(8,128)} %get-tuple-element.8) | copy-start | bytes 24580

commit v3 on v2

--- a/solution.py
+++ b/solution.py
@@ -22,6 +22,12 @@
 PAIRS = 1024
 STRIPS = (-1, 0, 1)
 OFFSETS = (-2, -1, 0, 1, 2)
+SPREAD = (
+    ((0, 24), (-1, 24), (1, 24), (-2, 16), (2, 16)),
+    ((0, 24), (-1, 24), (1, 24)),
+    ((0, 24), (-1, 16), (1, 16)),
+    ((0, 16),),
+)
 GROUPS = ("xc", "y", "z")
 PEERS = {"xc": 7, "y": 7, "z": 11}
 
@@ -128,6 +134,7 @@
     row_out,
     row_in,
     corner_in,
+    place_hot,
     depth_hot,
     first_hot,
     second_hot,
@@ -144,6 +151,18 @@
 ):
     lon, lat, block, inner = place()
     cn = {-2: c0, -1: c1, 0: c2, 1: c3, 2: c4}
+    barrier = pltpu.get_barrier_semaphore()
+    greeted = 0
+    for dl in OFFSETS:
+        for da in STRIPS:
+            if dl or da:
+                pl.semaphore_signal(
+                    barrier,
+                    inc=1,
+                    device_id=((lon + dl + LONS) % LONS, (lat + da + LATS) % LATS),
+                    device_id_type=MESH,
+                )
+                greeted += 1
     loads = []
     sources = [
         (courant, st_cn.at[0]),
@@ -163,25 +182,13 @@
         copy = pltpu.make_async_copy(src, dst, load_sem.at[i])
         copy.start()
         loads.append(copy)
-    barrier = pltpu.get_barrier_semaphore()
-    greeted = 0
-    for dl in OFFSETS:
-        for da in STRIPS:
-            if dl or da:
-                pl.semaphore_signal(
-                    barrier,
-                    inc=1,
-                    device_id=((lon + dl + LONS) % LONS, (lat + da + LATS) % LATS),
-                    device_id_type=MESH,
-                )
-                greeted += 1
     for group in GROUPS:
 
         def greet(r, carry, group=group):
             pl.semaphore_signal(barrier, inc=1, device_id=peer(group, r), device_id_type=MESH)
             return carry
 
-        lax.fori_loop(1, PEERS[group] + 1, greet, 0)
+        lax.fori_loop(1, PEERS[group] + 1, greet, 0, unroll=True)
         greeted += PEERS[group]
 
     lane = lax.broadcasted_iota(jnp.int32, (ROUND, 128), 1)
@@ -354,6 +361,8 @@
     for n in range(STEPS):
         for i in range(3):
             obs[3 * n + i : 3 * n + i + 1] = v_obs[i, n : n + 1]
+    for p in OFFSETS:
+        place_hot[p + 2] = jnp.where(spot == row_id + (p + 2) * ROUND, 1.0, 0.0)
     for j in range(8):
         chunks[j, 6:8] = jnp.zeros((2, 128), F32)
 
@@ -391,9 +400,7 @@
                 summed = jnp.zeros((ROUND, STATIONS), F32)
                 for k, p in enumerate(reach[n]):
                     at = (f * len(reach[n]) + k) * ROUND
-                    summed = summed + jnp.where(
-                        spot == row_id + (p + 2) * ROUND, picked[at : at + ROUND], 0.0
-                    )
+                    summed = summed + place_hot[p + 2] * picked[at : at + ROUND]
                 line = jnp.sum(summed, axis=0, keepdims=True)
                 chunks[2 * n + f, i : i + 1] = line[:, 0:128]
                 chunks[2 * n + f, 3 + i : 4 + i] = line[:, 128:256]
@@ -415,7 +422,7 @@
             ).start()
             return carry
 
-        lax.fori_loop(1, PEERS[group] + 1, one, 0)
+        lax.fori_loop(1, PEERS[group] + 1, one, 0, unroll=True)
 
     def drain(k, group, side):
         ref = slots.at[k % 3, pl.ds(0, PEERS[group])]
@@ -503,9 +510,6 @@
         step(2 * h, *now)
         step(2 * h + 1, *new)
 
-    two_steps(0)
-    halos.append(send_halo(1))
-
     shrink = (OFFSETS, (-1, 0, 1), (-1, 0, 1), (0,))
 
     def gather_sum(k, group, own_part):
@@ -519,11 +523,13 @@
     gather_sum(0, "xc", chunks[me_xc])
     post(1, "y", lambda r: total.at[0], lambda r: slots.at[1, r - 1])
 
+    two_steps(0)
+    halos.append(send_halo(1))
     gather_sum(1, "y", total[0])
     post(2, "z", lambda r: total.at[1], lambda r: slots.at[2, r - 1])
-    two_steps(1)
     gathered[me_xc] = gather_sum(2, "z", total[1])
     post(3, "xc", lambda r: total.at[2], lambda r: gathered.at[me_xc])
+    two_steps(1)
     ref = gathered.at[pl.ds(0, 7)]
     pltpu.make_async_copy(ref, ref, group_sem.at[1, 3]).wait()
 
@@ -550,28 +556,28 @@
     now = [{} for c in range(6)]
     old = [{} for c in range(6)]
     added = []
-    halves = [split2(v) for v in src]
+    halves = [[h.astype(F32) for h in split2(v)] for v in src]
     for k in range(STEPS):
         later = STEPS - 1 - k
         for c in range(6):
             new = advance(now[c], old[c], speed, shrink[k], lane) if k else {}
             old[c] = now[c]
             line = 3 * later + c % 3
-            lhs = []
+            parts = []
             for h in halves[c // 3]:
-                mine = jnp.broadcast_to(h[line : line + 1].astype(F32), (ROUND, STATIONS))
-                for p in shrink[k]:
-                    lhs.append(
-                        jnp.where(spot == row_id + (p + 2) * ROUND, mine, 0.0).astype(BF16)
-                    )
-            put = dot_t(jnp.concatenate(lhs, axis=0), hot)
-            count = len(shrink[k])
-            for j, p in enumerate(shrink[k]):
-                both = (
-                    put[j * ROUND : (j + 1) * ROUND]
-                    + put[(count + j) * ROUND : (count + j + 1) * ROUND]
-                )
-                new[p] = new[p] + both if k else both
+                mine = jnp.broadcast_to(h[line : line + 1], (ROUND, STATIONS))
+                for p, rows in SPREAD[k]:
+                    parts.append(place_hot[p + 2, 0:rows] * mine[0:rows])
+            put = dot_t(jnp.concatenate(parts, axis=0).astype(BF16), hot)
+            half = put.shape[0] // 2
+            both = put[0:half] + put[half:]
+            at = 0
+            for p, rows in SPREAD[k]:
+                piece = both[at : at + rows]
+                if rows < ROUND:
+                    piece = jnp.concatenate([piece, jnp.zeros((ROUND - rows, 128), F32)], axis=0)
+                new[p] = new[p] + piece if k else piece
+                at += rows
             now[c] = new
         added.append([now[c][0][0:ROWS] for c in range(6)])
 
@@ -598,6 +604,12 @@
                 copy.wait_send()
     for k, group in enumerate(("xc", "y", "z", "xc")):
         drain(k, group, 0)
+
+
+def hand_over(corr, adj, kernel, out_corr, out_adj, out_kernel):
+    out_corr[...] = corr[...]
+    out_adj[...] = adj[...]
+    out_kernel[...] = kernel[...]
 
 
 def shards(
@@ -618,7 +630,7 @@
     anywhere = pl.BlockSpec(memory_space=pltpu.HBM)
     vmem = pl.BlockSpec(memory_space=pltpu.VMEM)
     cn = pltpu.VMEM((2, ROUND, 128), F32)
-    return pl.pallas_call(
+    results = pl.pallas_call(
         body,
         name="window",
         out_shape=(
@@ -647,6 +659,7 @@
             pltpu.VMEM((2, 2, 3, 16, 128), F32),
             pltpu.VMEM((2, 2, 3, 16, 128), F32),
             pltpu.VMEM((2, 2, 2, 16, 128), F32),
+            pltpu.VMEM((5, ROUND, STATIONS), F32),
             pltpu.VMEM((256, STATIONS), BF16),
             pltpu.VMEM((STATIONS, PAIRS), BF16),
             pltpu.VMEM((STATIONS, PAIRS), BF16),
@@ -679,6 +692,14 @@
         jnp.transpose(observed, (1, 0, 2)),
         checkpoint,
     )
+    return pl.pallas_call(
+        hand_over,
+        name="results",
+        out_shape=tuple(jax.ShapeDtypeStruct(r.shape, r.dtype) for r in results),
+        in_specs=[vmem] * 3,
+        out_specs=(vmem,) * 3,
+        compiler_params=pltpu.CompilerParams(vmem_limit_bytes=56 * 1024 * 1024),
+    )(*results)
 
 
 def solution(mesh):

time: 53.3 us -> 51.6 us (0.968)
  local copies, waits for them, and re-layouts: 2.78 us -> 0 us
  Pallas kernels: 49 us -> 50.1 us
    unnamed x7 -> x0, local copies, waits for them, and re-layouts: 2.78 us -> none
    pallas_call x0 -> x1, Pallas kernels: none -> 1.56 us  [shards(): pl.pallas_call(hand_over, name='results', out_shape=tuple((jax.ShapeDtype...]
where the time goes in v3:
time: 51.6 us; the launch traced here: 51.4 us
  Pallas kernels  50.1 us (97%)
  between operations  1.29 us (2%)
    pallas_call x1, Pallas kernels, shards(): pl.pallas_call(body, name='window', out_shape=(jax.ShapeDtypeStruct((3, L...  48.5 us
    pallas_call x1, Pallas kernels, shards(): pl.pallas_call(hand_over, name='results', out_shape=tuple((jax.ShapeDtype...  1.56 us

profile of v3, /device:TPU:1, one launch (start us, length us, event | category | flops | bytes accessed | tf_op | source)
XLA Modules:
  0.0 51.4 jit_solution(14846304486384431131)
XLA Ops:
  1.3 48.5 %window.1 = (f32[3,2,16,64]{3,2,1,0:T(8,128)}, f32[6,2,16,64]{3,2,1,0:T(8,128)}, f32[2,16,64]{2,1,0:T(8,128)}) custom-call(f32[3,2,16,64]{3,2,1,0:T(8,128)} %gen_prev.1, f32[3,2,16,64]{3,2,1,0:T(8,128)} %gen_cur.1, f32[3,2,16,64]{3,2,1,0:T(8,128)} %corr_prev.1, f32[3,2,16,64]{3,2,1,0:T(8,128)} %corr_cur.1, f32[6,2,16,64]{3,2,1,0:T(8,128)} %adj_prev.1, ...), custom_call_target="tpu_custom_call" | custom-call | tf_op jit(solution)/shard_map/window/pallas_call | solution.py:633
  49.8 1.6 %results.1 = (f32[3,2,16,64]{3,2,1,0:T(8,128)}, f32[6,2,16,64]{3,2,1,0:T(8,128)}, f32[2,16,64]{2,1,0:T(8,128)}) custom-call(f32[3,2,16,64]{3,2,1,0:T(8,128)} %get-tuple-element.6.corr, f32[6,2,16,64]{3,2,1,0:T(8,128)} %get-tuple-element.7.adj, f32[2,16,64]{2,1,0:T(8,128)} %get-tuple-element.8.kernel), custom_call_target="tpu_custom_call" | custom-call | tf_op jit(solution)/shard_map/results/pallas_call | solution.py:695

commit v4 on v3

--- a/solution.py
+++ b/solution.py
@@ -28,8 +28,13 @@
     ((0, 24), (-1, 16), (1, 16)),
     ((0, 16),),
 )
-GROUPS = ("xc", "y", "z")
+GROUPS = ("z", "y", "xc")
 PEERS = {"xc": 7, "y": 7, "z": 11}
+ORDER = {
+    "xc": (4, 3, 5, 2, 6, 1, 7),
+    "y": (4, 3, 5, 2, 6, 1, 7),
+    "z": (6, 5, 7, 4, 8, 3, 9, 2, 10, 1, 11),
+}
 
 
 def place():
@@ -69,7 +74,7 @@
     return lax.dot_general(a, b, (((1,), (1,)), ((), ())), preferred_element_type=F32)
 
 
-def laplace(cur, p, lane):
+def around(cur, p, lane):
     x = cur.get(p)
     low = cur.get(p - 1)
     high = cur.get(p + 1)
@@ -84,15 +89,15 @@
     higher = jnp.where(lane % DEEP == DEEP - 1, 0.0, pltpu.roll(x, 127, 1))
     north = pltpu.roll(x, 1, 0)
     south = pltpu.roll(x, ROUND - 1, 0)
-    return along_lon + (north + south + deeper + higher) - 6.0 * x
-
-
-def advance(cur, old, speed, pairs, lane):
+    return along_lon + (north + south + deeper + higher)
+
+
+def advance(cur, old, speed, hold, pairs, lane):
     new = {}
     for p in pairs:
-        v = speed[p] * laplace(cur, p, lane)
+        v = speed[p] * around(cur, p, lane)
         if p in cur:
-            v = v + 2.0 * cur[p]
+            v = v + hold[p] * cur[p]
         if p in old:
             v = v - old[p]
         new[p] = v
@@ -163,6 +168,11 @@
                     device_id_type=MESH,
                 )
                 greeted += 1
+    for group in GROUPS:
+        for r in ORDER[group]:
+            pl.semaphore_signal(barrier, inc=1, device_id=peer(group, r), device_id_type=MESH)
+        greeted += PEERS[group]
+
     loads = []
     sources = [
         (courant, st_cn.at[0]),
@@ -182,15 +192,6 @@
         copy = pltpu.make_async_copy(src, dst, load_sem.at[i])
         copy.start()
         loads.append(copy)
-    for group in GROUPS:
-
-        def greet(r, carry, group=group):
-            pl.semaphore_signal(barrier, inc=1, device_id=peer(group, r), device_id_type=MESH)
-            return carry
-
-        lax.fori_loop(1, PEERS[group] + 1, greet, 0, unroll=True)
-        greeted += PEERS[group]
-
     lane = lax.broadcasted_iota(jnp.int32, (ROUND, 128), 1)
     sub8 = lax.broadcasted_iota(jnp.int32, (8, 128), 0)
     zeros8 = jnp.zeros((8, 128), F32)
@@ -279,11 +280,31 @@
         copies = []
         for d, dl in enumerate((-1, 1)):
             copies.append(
-                (remote(side_out.at[h, d], side_in.at[h, d], halo_sem.at[h], len(copies), dl, 0), 0)
+                (
+                    remote(
+                        side_out.at[h, d, pl.ds(0, 3 - h)],
+                        side_in.at[h, d, pl.ds(0, 3 - h)],
+                        halo_sem.at[h],
+                        len(copies),
+                        dl,
+                        0,
+                    ),
+                    0,
+                )
             )
         for d, da in enumerate((-1, 1)):
             copies.append(
-                (remote(row_out.at[h, d], row_in.at[h, d], halo_sem.at[h], len(copies), 0, da), da)
+                (
+                    remote(
+                        row_out.at[h, d, pl.ds(0, 3 - h)],
+                        row_in.at[h, d, pl.ds(0, 3 - h)],
+                        halo_sem.at[h],
+                        len(copies),
+                        0,
+                        da,
+                    ),
+                    da,
+                )
             )
         for d, da in enumerate((-1, 1)):
             for e, dl in enumerate((-1, 1)):
@@ -314,17 +335,20 @@
             side_out[h, 1, 0, c] = jnp.where(lane16 < DEEP, two_t, one)
             side_out[h, 0, 1, c] = jnp.where(lane16 < DEEP, one_t, two)
             side_out[h, 1, 1, c] = jnp.where(lane16 < DEEP, two, one_t)
-            one, two_t = fields[n - 1, c], turn(fields[n - 1, c + 6])
-            side_out[h, 0, 2, c] = jnp.where(lane16 < DEEP, one, two_t)
-            side_out[h, 1, 2, c] = jnp.where(lane16 < DEEP, two_t, one)
+            if h == 0:
+                one, two_t = fields[n - 1, c], turn(fields[n - 1, c + 6])
+                side_out[h, 0, 2, c] = jnp.where(lane16 < DEEP, one, two_t)
+                side_out[h, 1, 2, c] = jnp.where(lane16 < DEEP, two_t, one)
         for c in range(12):
-            now, before = fields[n, c], fields[n - 1, c]
+            now = fields[n, c]
             row_out[h, 0, 0, c : c + 1] = now[0:1]
             row_out[h, 0, 1, c : c + 1] = now[1:2]
-            row_out[h, 0, 2, c : c + 1] = before[0:1]
             row_out[h, 1, 0, c : c + 1] = now[ROWS - 1 : ROWS]
             row_out[h, 1, 1, c : c + 1] = now[ROWS - 2 : ROWS - 1]
-            row_out[h, 1, 2, c : c + 1] = before[ROWS - 1 : ROWS]
+            if h == 0:
+                before = fields[n - 1, c]
+                row_out[h, 0, 2, c : c + 1] = before[0:1]
+                row_out[h, 1, 2, c : c + 1] = before[ROWS - 1 : ROWS]
         copies = halo(h)
         go(copies)
         return copies
@@ -350,8 +374,8 @@
     depth_hot[0:128] = hot
     depth_hot[128:256] = hot
 
-    phase = checkpoint[0].astype(F32)
-    weights = [jnp.cos(jnp.full((ROUND, 128), OMEGA * (phase + n), F32)) for n in range(STEPS)]
+    phase = jnp.broadcast_to(checkpoint[...], (8, 128)).astype(F32)
+    weights = [jnp.tile(jnp.cos(OMEGA * (phase + n)), (ROUND // 8, 1)) for n in range(STEPS)]
 
     ids = lax.broadcasted_iota(jnp.int32, (STATIONS, PAIRS), 0)
     first_hot[...] = jnp.where(ids == v_pairs[0:1], 1.0, 0.0).astype(BF16)
@@ -374,23 +398,26 @@
             cn[p][ch, ROWS:ROUND] = jnp.where(sub8 < 4, above, below)
     reach = ((-1, 0, 1), (-1, 0, 1), OFFSETS, OFFSETS)
 
+    speed = {p: cn[p][0] for p in OFFSETS}
+    hold = {p: 2.0 - 6.0 * speed[p] for p in OFFSETS}
+    noisy = [{p: cn[p][1] * weights[n] for p in reach[n]} for n in range(STEPS)]
+
     def responses(i):
         pad = jnp.zeros((8, 128), F32)
 
         def own_cells(t, ch):
             return jnp.concatenate([fields[1 - t, ch], pad], axis=0)
 
-        speed = {p: cn[p][0] for p in OFFSETS}
         gen = {0: own_cells(0, i)}
         gen_old = {0: own_cells(1, i)}
         corr = {0: own_cells(0, 3 + i)}
         corr_old = {0: own_cells(1, 3 + i)}
         for n in range(STEPS):
-            gen_new = advance(gen, gen_old, speed, reach[n], lane)
-            corr_new = advance(corr, corr_old, speed, reach[n], lane)
+            gen_new = advance(gen, gen_old, speed, hold, reach[n], lane)
+            corr_new = advance(corr, corr_old, speed, hold, reach[n], lane)
             for p in reach[n]:
                 if p in gen:
-                    corr_new[p] = corr_new[p] + (cn[p][1] * weights[n]) * gen[p]
+                    corr_new[p] = corr_new[p] + noisy[n][p] * gen[p]
             gen_old, gen = gen, gen_new
             corr_old, corr = corr, corr_new
             tiles = [field[p] for field in (gen, corr) for p in reach[n]]
@@ -411,7 +438,7 @@
     me_xc = block % 4 * 2 + inner % 2
 
     def post(k, group, src_of, dst_of):
-        def one(r, carry):
+        for r in ORDER[group]:
             pltpu.make_async_remote_copy(
                 src_of(r),
                 dst_of(r),
@@ -420,9 +447,6 @@
                 device_id=peer(group, r),
                 device_id_type=MESH,
             ).start()
-            return carry
-
-        lax.fori_loop(1, PEERS[group] + 1, one, 0, unroll=True)
 
     def drain(k, group, side):
         ref = slots.at[k % 3, pl.ds(0, PEERS[group])]
@@ -457,12 +481,18 @@
                 new = new + noisy * fields[n + 1, c - 3]
             fields[n + 2, c] = new
 
-    def layer(h):
+    def layer(h, before):
         n = 2 * h
         arrived = (has_low, has_high)
         row = [
-            [jnp.where(arrived[d], row_in[h, 1 - d, j], 0.0) for j in range(3)] for d in range(2)
+            [jnp.where(arrived[d], row_in[h, 1 - d, j], 0.0) for j in range(3 - h)]
+            for d in range(2)
         ]
+        if before is None:
+            before = (
+                [[side_in[h, 1 - e, 2, c] for c in range(6)] for e in range(2)],
+                [row[d][2] for d in range(2)],
+            )
         corner = [
             [jnp.where(arrived[d], corner_in[h, 1 - d, 1 - e], 0.0) for e in range(2)]
             for d in range(2)
@@ -485,7 +515,7 @@
                 along_lon = side_in[h, 1 - e, 1, c] + side_out[h, 1 - e, 1, c]
                 near = lat_sum(x, ends[0][c : c + 1], ends[1][c : c + 1])
                 around = along_lon + (near + depth_sum(x, lane16)) - 6.0 * x
-                v = 2.0 * x - side_in[h, 1 - e, 2, c] + speed * around
+                v = 2.0 * x - before[0][e][c] + speed * around
                 if c >= 3:
                     v = v + noisy * sides_now[e][c - 3]
                 new.append(v)
@@ -498,17 +528,18 @@
             sides = jnp.where(lane16 < DEEP, corner[d][1], corner[d][0])
             own = row_out[h, d, 0]
             around = turn(x + sides) + (own + row[d][1] + depth_sum(x, lane16)) - 6.0 * x
-            v = 2.0 * x - row[d][2] + c2[0, at : at + 1] * around
+            v = 2.0 * x - before[1][d] + c2[0, at : at + 1] * around
             moved = jnp.where((row16 >= 3) & (row16 < 6), pltpu.roll(x, 3, 0), 0.0)
             v = v + (c2[1, at : at + 1] * weights[n][0:1]) * moved
             rows_new.append(v)
         return (sides_now, rows_now), (sides_new, rows_new)
 
-    def two_steps(h):
+    def two_steps(h, before):
         take(halos[h])
-        now, new = layer(h)
+        now, new = layer(h, before)
         step(2 * h, *now)
         step(2 * h + 1, *new)
+        return new
 
     shrink = (OFFSETS, (-1, 0, 1), (-1, 0, 1), (0,))
 
@@ -523,13 +554,13 @@
     gather_sum(0, "xc", chunks[me_xc])
     post(1, "y", lambda r: total.at[0], lambda r: slots.at[1, r - 1])
 
-    two_steps(0)
+    kept = two_steps(0, None)
     halos.append(send_halo(1))
     gather_sum(1, "y", total[0])
     post(2, "z", lambda r: total.at[1], lambda r: slots.at[2, r - 1])
     gathered[me_xc] = gather_sum(2, "z", total[1])
     post(3, "xc", lambda r: total.at[2], lambda r: gathered.at[me_xc])
-    two_steps(1)
+    two_steps(1, kept)
     ref = gathered.at[pl.ds(0, 7)]
     pltpu.make_async_copy(ref, ref, group_sem.at[1, 3]).wait()
 
@@ -551,7 +582,6 @@
     misfit = gen_a * corr_b - obs[...]
     src = (thirds(misfit * corr_b, first, dot_t), thirds(misfit * gen_a, second, dot_t))
 
-    speed = {p: cn[p][0] for p in OFFSETS}
     hot = depth_hot[0:128]
     now = [{} for c in range(6)]
     old = [{} for c in range(6)]
@@ -560,7 +590,7 @@
     for k in range(STEPS):
         later = STEPS - 1 - k
         for c in range(6):
-            new = advance(now[c], old[c], speed, shrink[k], lane) if k else {}
+            new = advance(now[c], old[c], speed, hold, shrink[k], lane) if k else {}
             old[c] = now[c]
             line = 3 * later + c % 3
             parts = []
@@ -638,7 +668,7 @@
             jax.ShapeDtypeStruct((6, LONG, ROWS, DEEP), F32),
             jax.ShapeDtypeStruct((LONG, ROWS, DEEP), F32),
         ),
-        in_specs=[anywhere] * 12 + [pl.BlockSpec(memory_space=pltpu.SMEM)],
+        in_specs=[anywhere] * 12 + [vmem],
         out_specs=(vmem, vmem, vmem),
         scratch_shapes=[
             pltpu.VMEM((2, 12, LONG, ROWS, DEEP), F32),
@@ -690,7 +720,7 @@
         station_cell.reshape(1, STATIONS),
         pairs,
         jnp.transpose(observed, (1, 0, 2)),
-        checkpoint,
+        checkpoint.reshape(1, 1),
     )
     return pl.pallas_call(
         hand_over,

time: 51.6 us -> 51.3 us (level)
  no operation moved by 1% of the time
where the time goes in v4:
time: 51.3 us; the launch traced here: 51.1 us
  Pallas kernels  49.8 us (97%)
  between operations  1.29 us (3%)
    pallas_call x1, Pallas kernels, shards(): pl.pallas_call(body, name='window', out_shape=(jax.ShapeDtypeStruct((3, L...  48.2 us
    pallas_call x1, Pallas kernels, shards(): pl.pallas_call(hand_over, name='results', out_shape=tuple((jax.ShapeDtype...  1.56 us

profile of v4, /device:TPU:1, one launch (start us, length us, event | category | flops | bytes accessed | tf_op | source)
XLA Modules:
  0.0 51.1 jit_solution(17023211971555080914)
XLA Ops:
  1.3 48.2 %window.1 = (f32[3,2,16,64]{3,2,1,0:T(8,128)}, f32[6,2,16,64]{3,2,1,0:T(8,128)}, f32[2,16,64]{2,1,0:T(8,128)}) custom-call(f32[3,2,16,64]{3,2,1,0:T(8,128)} %gen_prev.1, f32[3,2,16,64]{3,2,1,0:T(8,128)} %gen_cur.1, f32[3,2,16,64]{3,2,1,0:T(8,128)} %corr_prev.1, f32[3,2,16,64]{3,2,1,0:T(8,128)} %corr_cur.1, f32[6,2,16,64]{3,2,1,0:T(8,128)} %adj_prev.1, ...), custom_call_target="tpu_custom_call" | custom-call | tf_op jit(solution)/shard_map/window/pallas_call | solution.py:663
  49.5 1.6 %results.1 = (f32[3,2,16,64]{3,2,1,0:T(8,128)}, f32[6,2,16,64]{3,2,1,0:T(8,128)}, f32[2,16,64]{2,1,0:T(8,128)}) custom-call(f32[3,2,16,64]{3,2,1,0:T(8,128)} %get-tuple-element.6.corr, f32[6,2,16,64]{3,2,1,0:T(8,128)} %get-tuple-element.7.adj, f32[2,16,64]{2,1,0:T(8,128)} %get-tuple-element.8.kernel), custom_call_target="tpu_custom_call" | custom-call | tf_op jit(solution)/shard_map/results/pallas_call | solution.py:725

commit v5 on v4

--- a/solution.py
+++ b/solution.py
@@ -57,13 +57,6 @@
 def split2(v):
     high = v.astype(BF16)
     return high, (v - high.astype(F32)).astype(BF16)
-
-
-def split3(v):
-    high = v.astype(BF16)
-    rest = v - high.astype(F32)
-    mid = rest.astype(BF16)
-    return high, mid, (rest - mid.astype(F32)).astype(BF16)
 
 
 def dot(a, b):
@@ -387,8 +380,6 @@
             obs[3 * n + i : 3 * n + i + 1] = v_obs[i, n : n + 1]
     for p in OFFSETS:
         place_hot[p + 2] = jnp.where(spot == row_id + (p + 2) * ROUND, 1.0, 0.0)
-    for j in range(8):
-        chunks[j, 6:8] = jnp.zeros((2, 128), F32)
 
     take(cn_copies)
     for p in OFFSETS:
@@ -436,6 +427,7 @@
         responses(i)
 
     me_xc = block % 4 * 2 + inner % 2
+    held = pl.ds(0, 6)
 
     def post(k, group, src_of, dst_of):
         for r in ORDER[group]:
@@ -449,10 +441,10 @@
             ).start()
 
     def drain(k, group, side):
-        ref = slots.at[k % 3, pl.ds(0, PEERS[group])]
+        ref = slots.at[k % 3, pl.ds(0, PEERS[group]), held]
         pltpu.make_async_copy(ref, ref, group_sem.at[side, k]).wait()
 
-    post(0, "xc", lambda r: chunks.at[(me_xc + r) % 8], lambda r: slots.at[0, r - 1])
+    post(0, "xc", lambda r: chunks.at[(me_xc + r) % 8, held], lambda r: slots.at[0, r - 1, held])
 
     def depth_sum(x, lanes):
         deeper = jnp.where(lanes % DEEP == 0, 0.0, pltpu.roll(x, 1, 1))
@@ -547,21 +539,21 @@
         drain(k, group, 1)
         part = own_part
         for r in range(PEERS[group]):
-            part = part + slots[k, r]
-        total[k] = part
+            part = part + slots[k, r, 0:6]
+        total[k, 0:6] = part
         return part
 
-    gather_sum(0, "xc", chunks[me_xc])
-    post(1, "y", lambda r: total.at[0], lambda r: slots.at[1, r - 1])
+    gather_sum(0, "xc", chunks[me_xc, 0:6])
+    post(1, "y", lambda r: total.at[0, held], lambda r: slots.at[1, r - 1, held])
 
     kept = two_steps(0, None)
     halos.append(send_halo(1))
-    gather_sum(1, "y", total[0])
-    post(2, "z", lambda r: total.at[1], lambda r: slots.at[2, r - 1])
-    gathered[me_xc] = gather_sum(2, "z", total[1])
-    post(3, "xc", lambda r: total.at[2], lambda r: gathered.at[me_xc])
+    gather_sum(1, "y", total[0, 0:6])
+    post(2, "z", lambda r: total.at[1, held], lambda r: slots.at[2, r - 1, held])
+    gathered[me_xc, 0:6] = gather_sum(2, "z", total[1, 0:6])
+    post(3, "xc", lambda r: total.at[2, held], lambda r: gathered.at[me_xc, held])
     two_steps(1, kept)
-    ref = gathered.at[pl.ds(0, 7)]
+    ref = gathered.at[pl.ds(0, 7), held]
     pltpu.make_async_copy(ref, ref, group_sem.at[1, 3]).wait()
 
     for n in range(STEPS):
@@ -570,17 +562,17 @@
             rec[f, 3 * n : 3 * n + 3, 0:128] = tile[0:3]
             rec[f, 3 * n : 3 * n + 3, 128:256] = tile[3:6]
 
-    def thirds(v, hot, times):
-        stack = jnp.concatenate(split3(v), axis=0)
+    def parted(v, hot, times):
+        stack = jnp.concatenate(split2(v), axis=0)
         got = times(stack, hot)
-        return got[0:16] + got[16:32] + got[32:48]
+        return got[0:16] + got[16:32]
 
     first = first_hot[...]
     second = second_hot[...]
-    gen_a = thirds(rec[0], first, dot)
-    corr_b = thirds(rec[1], second, dot)
+    gen_a = parted(rec[0], first, dot)
+    corr_b = parted(rec[1], second, dot)
     misfit = gen_a * corr_b - obs[...]
-    src = (thirds(misfit * corr_b, first, dot_t), thirds(misfit * gen_a, second, dot_t))
+    src = (parted(misfit * corr_b, first, dot_t), parted(misfit * gen_a, second, dot_t))
 
     hot = depth_hot[0:128]
     now = [{} for c in range(6)]

time: 51.3 us -> 51.1 us (level)
  no operation moved by 1% of the time
where the time goes in v5:
time: 51.1 us; the launch traced here: 50.9 us
  Pallas kernels  49.6 us (97%)
  between operations  1.29 us (3%)
    pallas_call x1, Pallas kernels, shards(): pl.pallas_call(body, name='window', out_shape=(jax.ShapeDtypeStruct((3, L...  48 us
    pallas_call x1, Pallas kernels, shards(): pl.pallas_call(hand_over, name='results', out_shape=tuple((jax.ShapeDtype...  1.56 us

profile of v5, /device:TPU:1, one launch (start us, length us, event | category | flops | bytes accessed | tf_op | source)
XLA Modules:
  0.0 50.9 jit_solution(5527149006855488281)
XLA Ops:
  1.3 48.0 %window.1 = (f32[3,2,16,64]{3,2,1,0:T(8,128)}, f32[6,2,16,64]{3,2,1,0:T(8,128)}, f32[2,16,64]{2,1,0:T(8,128)}) custom-call(f32[3,2,16,64]{3,2,1,0:T(8,128)} %gen_prev.1, f32[3,2,16,64]{3,2,1,0:T(8,128)} %gen_cur.1, f32[3,2,16,64]{3,2,1,0:T(8,128)} %corr_prev.1, f32[3,2,16,64]{3,2,1,0:T(8,128)} %corr_cur.1, f32[6,2,16,64]{3,2,1,0:T(8,128)} %adj_prev.1, ...), custom_call_target="tpu_custom_call" | custom-call | tf_op jit(solution)/shard_map/window/pallas_call | solution.py:655
  49.3 1.6 %results.1 = (f32[3,2,16,64]{3,2,1,0:T(8,128)}, f32[6,2,16,64]{3,2,1,0:T(8,128)}, f32[2,16,64]{2,1,0:T(8,128)}) custom-call(f32[3,2,16,64]{3,2,1,0:T(8,128)} %get-tuple-element.6.corr, f32[6,2,16,64]{3,2,1,0:T(8,128)} %get-tuple-element.7.adj, f32[2,16,64]{2,1,0:T(8,128)} %get-tuple-element.8.kernel), custom_call_target="tpu_custom_call" | custom-call | tf_op jit(solution)/shard_map/results/pallas_call | solution.py:717
